TPU v7x, 128 devices: a whole 4x4x4 slice. The times are simulated.
128 devices in a mesh: sec: 2 (over z_lo), gx: 8 (over x, core), gy: 8 (over z_hi, y).
Axes of the slice: x: 4, y: 4, z: 4 (z_hi: 2, z_lo: 2; z = z_hi * 2 + z_lo), core: 2. Of those that a mesh axis runs over, the one named last changes fastest.
Arguments:
- state: float32 [4, 16, 1280, 2560], P(None, None, ('gx', 'gy'), 'sec'), may hold values from -6 to 6
- h_coeff: float32 [4, 16], replicated, may hold values from 0.03 to 0.12
- v_coeff: float32 [4, 16], replicated, may hold values from 0.03 to 0.15
- conv_weight: bfloat16 [4, 5, 5, 32], replicated, may hold values from -0.625 to 0.625
- conv_bias: float32 [32], replicated, may hold values from -3 to 3
- readout: float32 [32, 2], replicated, may hold values from -1 to 1
- readout_bias: float32 [2], replicated, may hold values from -2 to 2
- level_base: int32 [2, 256, 512], P(None, 'gx', ('sec', 'gy')), may hold values from 0 to 7
- level_depth: int32 [2, 256, 512], P(None, 'gx', ('sec', 'gy')), may hold values from 1 to 8
Outputs:
- advanced: float32 [4, 16, 1280, 2560], P(None, None, ('gx', 'gy'), 'sec')
- column_fraction: float32 [2, 256, 512], P(None, 'gx', ('sec', 'gy'))
- area_fraction: float32 [2, 256, 512], P(None, 'gx', ('sec', 'gy'))
All inputs are finite; a program needn't handle non-finite values.
Results may differ from a plain program's by a relative error of at most 0.00033.
Values may be sent and summed in bfloat16 or wider, within the bound.
A program may use at most 384 MiB of HBM per device.

v0:
```python
import jax
import jax.numpy as jnp
from jax import lax
from jax.sharding import PartitionSpec as P

KERNEL = 5
WIN = 24


def extended_2(block, sides, width):
    for axis, dim in sides:
        count = lax.axis_size(axis)
        forward = [(i, i + 1) for i in range(count - 1)]
        forward.append((count - 1, 0))
        backward = [(target, source) for source, target in forward]
        low = lax.ppermute(
            lax.slice_in_dim(block, block.shape[dim] - width, None, axis=dim), axis, forward
        )
        high = lax.ppermute(lax.slice_in_dim(block, 0, width, axis=dim), axis, backward)
        block = jnp.concatenate([low, block, high], axis=dim)
    return block


def fourth(block, dim):
    count = block.shape[dim] - 4

    def part(offset):
        return lax.slice_in_dim(block, offset, offset + count, axis=dim)

    return (16.0 * (part(1) + part(3)) - (part(0) + part(4)) - 30.0 * part(2)) / 12.0


def sweep(block, horiz, vertical):
    center = block[:, :, 2:-2, 2:-2]
    laplace = fourth(block[:, :, :, 2:-2], 2) + fourth(block[:, :, 2:-2, :], 3)
    padded = jnp.pad(center, ((0, 0), (1, 1), (0, 0), (0, 0)))
    vert = padded[:, 2:] + padded[:, :-2] - 2.0 * center
    return center + horiz * laplace + vertical * vert


def column_probs(fields, conv_weight, conv_bias, readout, readout_bias):
    count_f, count_l, width_x, width_y = fields.shape
    blocks = fields.reshape(count_f, count_l, width_x // KERNEL, KERNEL, width_y // KERNEL, KERNEL)
    feats = jnp.einsum("flpaqb,fabk->lkpq", blocks, conv_weight, preferred_element_type=jnp.float32)
    feats = jnp.maximum(feats + conv_bias[None, :, None, None], 0.0)
    score = jnp.einsum("lkpq,kc->clpq", feats, readout, precision=lax.Precision.HIGHEST)
    return jax.nn.sigmoid(score + readout_bias[:, None, None, None])


def band_matrix(count):
    rows_idx = jnp.arange(count, dtype=jnp.int32)[:, None]
    cols_idx = jnp.arange(count + WIN, dtype=jnp.int32)[None, :]
    offset = cols_idx - rows_idx
    return ((offset >= 0) & (offset < WIN)).astype(jnp.float32)


def window_mean(wide, count_x, count_y):
    band_x = band_matrix(count_x)
    band_y = band_matrix(count_y)
    rows_sum = jnp.einsum("ij,cjk->cik", band_x, wide, precision=lax.Precision.HIGHEST)
    both_sum = jnp.einsum("cik,lk->cil", rows_sum, band_y, precision=lax.Precision.HIGHEST)
    return both_sum / float(WIN * WIN)


def on_device(
    state, h_coeff, v_coeff, conv_weight, conv_bias, readout, readout_bias, level_base, level_depth
):
    horiz = h_coeff[:, :, None, None]
    vertical = v_coeff[:, :, None, None]
    current = state
    for sweep_index in range(2):
        extended = extended_2(current, ((("gx", "gy"), 2), ("sec", 3)), 2)
        current = sweep(extended, horiz, vertical)
    rounded = current.astype(jnp.bfloat16)
    prob = column_probs(
        lax.all_to_all(rounded, "gy", split_axis=3, concat_axis=2, tiled=True),
        conv_weight,
        conv_bias,
        readout,
        readout_bias,
    )
    levels = prob.shape[1]
    level_now = jnp.arange(levels, dtype=jnp.int32)[None, :, None, None]
    inside = (level_now >= level_base[:, None]) & (level_now < (level_base + level_depth)[:, None])
    summed = jnp.sum(jnp.where(inside, prob, 0.0), axis=1)
    column_fraction = summed / level_depth.astype(jnp.float32)
    wide = extended_2(column_fraction, (("gx", 1), (("sec", "gy"), 2)), WIN // 2)
    area_fraction = window_mean(wide, column_fraction.shape[1], column_fraction.shape[2])
    return (current, column_fraction, area_fraction)


def solution(mesh):
    in_specs = (
        P(None, None, ("gx", "gy"), "sec"),
        P(),
        P(),
        P(),
        P(),
        P(),
        P(),
        P(None, "gx", ("sec", "gy")),
        P(None, "gx", ("sec", "gy")),
    )
    out_specs = (
        P(None, None, ("gx", "gy"), "sec"),
        P(None, "gx", ("sec", "gy")),
        P(None, "gx", ("sec", "gy")),
    )
    return jax.shard_map(
        on_device, mesh=mesh, in_specs=in_specs, out_specs=out_specs, check_vma=False
    )
```

profile of v0, /device:TPU:0, one launch (start us, length us, event | category | flops | bytes accessed | tf_op | source)
XLA Modules:
  0.0 485.4 jit_solution(2744416689112773227)
XLA Ops:
  0.6 0.0 copy-start
  0.6 1.4 fusion.95
  2.1 1.7 collective-permute-start
  3.8 6.5 %collective-permute-start.1 = (f32[4,16,2,1280]{3,1,2,0:T(8,128)S(1)}, f32[4,16,2,1280]{3,1,2,0:T(8,128)S(1)}, u32[]{:S(2)}, u32[]{:S(2)}) collective-permute-start(f32[4,16,2,1280]{3,1,2,0:T(8,128)S(1)} %get-tuple-element.22), channel_id=1, source_target_pairs={{1,0},{2,1},{3,2},{4,3},{5,4},{6,5},{7,6},{8,7},{9,8},{10,9},{11,1... | collective-permute-start | bytes 1966088 | tf_op jit(solution)/shard_map/ppermute | solution.py:19
  10.3 8.3 %collective-permute-done = f32[4,16,2,1280]{3,1,2,0:T(8,128)S(1)} collective-permute-done((f32[4,16,2,1280]{3,1,2,0:T(8,128)S(1)}, f32[4,16,2,1280]{3,1,2,0:T(8,128)S(1)}, u32[]{:S(2)}, u32[]{:S(2)}) %collective-permute-start) | collective-permute-done | bytes 655392 | tf_op jit(solution)/shard_map/ppermute | solution.py:16
  18.6 1.2 constant_dynamic-update-slice_fusion.1
  19.8 12.0 %constant_dynamic-update-slice_fusion = (f32[4,16,22,1280]{3,1,2,0:T(8,128)}, f32[4,16,22,1280]{3,1,2,0:T(8,128)}, f32[4,16,24,1280]{3,1,2,0:T(8,128)}) fusion(f32[4,16,22,1280]{3,1,2,0:T(8,128)} %get-tuple-element.24, f32[4,16,20,1280]{3,1,2,0:T(8,128)} %param.9, f32[4,16,24,1280]{3,1,2,0:T(8,128)} %get-tuple-element.25), kind=kLoop, calls=%fused_computation.88 | loop fusion | bytes 26214400 | tf_op jit(solution)/shard_map/concatenate | solution.py:20
  31.8 0.0 collective-permute-done.1
  31.8 1.2 constant_dynamic-update-slice_fusion.2
  33.0 1.7 fusion.93
  34.6 0.5 copy.96
  35.1 1.5 collective-permute-start.3
  36.6 0.5 copy.94
  37.1 0.7 collective-permute-start.2
  37.7 0.0 copy-done.8
  37.7 1.7 collective-permute-done.3
  39.4 0.5 copy.97
  39.9 1.5 collective-permute-done.2
  41.4 0.5 copy.95
  41.9 0.0 copy-done.7
  41.9 29.0 %fusion.22 = f32[4,16,20,1280]{3,1,2,0:T(8,128)S(1)} fusion(f32[4,16,20,1280]{3,1,2,0:T(8,128)} %param.9, f32[4,16,24,1280]{3,1,2,0:T(8,128)} %get-tuple-element.27, f32[4,16,24,2]{3,1,2,0:T(8,128)S(1)} %copy.97, f32[4,16,24,2]{3,1,2,0:T(8,128)S(1)} %copy.95, f32[4,16,22,1280]{3,1,2,0:T(8,128)} %get-tuple-element.26, ...), kind=kLoop, calls=%fused_computation.36 | loop fusion | flops 37683200 | bytes 47211008 | tf_op jit(solution)/shard_map/add | solution.py:38
  70.9 0.0 copy-start.1
  70.9 0.1 fusion.94
  71.0 6.9 %collective-permute-start.5 = (f32[4,16,2,1280]{3,1,2,0:T(8,128)S(1)}, f32[4,16,2,1280]{3,1,2,0:T(8,128)S(1)}, u32[]{:S(2)}, u32[]{:S(2)}) collective-permute-start(f32[4,16,2,1280]{3,1,2,0:T(8,128)S(1)} %get-tuple-element.18), channel_id=1, source_target_pairs={{1,0},{2,1},{3,2},{4,3},{5,4},{6,5},{7,6},{8,7},{9,8},{10,9},{11,1... | collective-permute-start | bytes 1966088 | tf_op jit(solution)/shard_map/ppermute | solution.py:19
  77.9 0.0 collective-permute-start.4
  77.9 8.5 %collective-permute-done.5 = f32[4,16,2,1280]{3,1,2,0:T(8,128)S(1)} collective-permute-done((f32[4,16,2,1280]{3,1,2,0:T(8,128)S(1)}, f32[4,16,2,1280]{3,1,2,0:T(8,128)S(1)}, u32[]{:S(2)}, u32[]{:S(2)}) %collective-permute-start.5) | collective-permute-done | bytes 655392 | tf_op jit(solution)/shard_map/ppermute | solution.py:19
  86.4 7.4 %collective-permute-done.4 = f32[4,16,2,1280]{3,1,2,0:T(8,128)S(1)} collective-permute-done((f32[4,16,2,1280]{3,1,2,0:T(8,128)S(1)}, f32[4,16,2,1280]{3,1,2,0:T(8,128)S(1)}, u32[]{:S(2)}, u32[]{:S(2)}) %collective-permute-start.4) | collective-permute-done | bytes 655392 | tf_op jit(solution)/shard_map/ppermute | solution.py:16
  93.8 0.0 copy-done.1
  93.8 0.3 pad_maximum_fusion.7
  94.0 0.5 copy.98
  94.5 0.1 collective-permute-start.6
  94.6 0.5 copy.100
  95.1 2.2 collective-permute-start.7
  97.3 1.5 collective-permute-done.6
  98.8 0.5 copy.99
  99.3 0.2 collective-permute-done.7
  99.6 0.5 copy.101
  100.0 12.5 %maximum_maximum_fusion = (f32[4,16,24,1282]{3,1,2,0:T(8,128)}, f32[4,16,24,1282]{3,1,2,0:T(8,128)}) fusion(f32[4,16,2,1280]{3,1,2,0:T(8,128)S(1)} %collective-permute-done.5, f32[4,16,20,1280]{3,1,2,0:T(8,128)} %copy-done.1, f32[4,16,2,1280]{3,1,2,0:T(8,128)S(1)} %collective-permute-done.4, f32[4,16,24,2]{3,1,2,0:T(8,128)S(1)} %copy.99, ...), kind=kLoop, calls=%fused_computation.8 | loop fusion | flops 11814912 | bytes 23642112 | tf_op jit(solution)/shard_map/concatenate | solution.py:20
  112.5 0.0 copy-done.2
  112.5 0.0 copy-done.3
  112.5 33.8 %fusion.91 = (bf16[4,16,20,1280]{3,1,2,0:T(8,128)(2,1)S(1)}, f32[4,16,20,1280]{3,1,2,0:T(8,128)}) fusion(f32[4,16,20,1280]{3,1,2,0:T(8,128)} %copy-done.1, f32[4,16]{1,0:T(4,128)S(1)} %copy-done.7, f32[4,16]{1,0:T(4,128)S(1)} %broadcast_multiply_fusion, f32[4,16,24,1282]{3,1,2,0:T(8,128)} %get-tuple-element.12, f32[4,16,24,1282]{3,1,2,0:T(8,128)} %get-tuple-element.11, ...), kind=kLoop, calls=%fused_computation.112 | loop fusion | flops 39321600 | bytes 43909632 | tf_op jit(solution)/shard_map/convert_element_type | solution.py:74
  146.3 17.4 %copy.104 = bf16[4,16,20,1280]{2,1,0,3:T(8,128)(2,1)} copy(bf16[4,16,20,1280]{3,1,2,0:T(8,128)(2,1)S(1)} %get-tuple-element.9) | data formatting | bytes 6553600 | tf_op jit(solution)/shard_map/convert_element_type | solution.py:74
  163.7 48.8 %reshape.21 = bf16[8,2,102400]{2,1,0:T(2,128)(2,1)} reshape(bf16[1280,4,16,20]{3,2,1,0:T(8,128)(2,1)} %bitcast.75) | data formatting | bytes 6553600
  212.5 6.5 %all-to-all-start = ((bf16[8,2,102400]{2,1,0:T(2,128)(2,1)}), bf16[8,2,102400]{2,1,0:T(2,128)(2,1)S(1)}, u32[]{:S(2)}, u32[]{:S(2)}) async-start(bf16[8,2,102400]{2,1,0:T(2,128)(2,1)} %reshape.21), calls=%async_computation | async-start | bytes 6553600 | tf_op jit(solution)/shard_map/all_to_all | solution.py:76
  219.1 42.2 %all-to-all-done = bf16[8,2,102400]{2,1,0:T(2,128)(2,1)S(1)} async-done(((bf16[8,2,102400]{2,1,0:T(2,128)(2,1)}), bf16[8,2,102400]{2,1,0:T(2,128)(2,1)S(1)}, u32[]{:S(2)}, u32[]{:S(2)}) %all-to-all-start) | async-done | bytes 3276832 | tf_op jit(solution)/shard_map/all_to_all | solution.py:76
  261.3 55.6 %reshape.22 = bf16[1280,4,16,20]{3,2,1,0:T(8,128)(2,1)} reshape(bf16[8,2,102400]{2,1,0:T(2,128)(2,1)S(1)} %all-to-all-done) | data formatting | bytes 6553600
  316.9 49.4 %copy.105 = bf16[4,16,20,8,160]{1,0,4,2,3:T(4,128)(2,1)} copy(bf16[4,16,20,8,160]{2,1,0,4,3:T(8,128)(2,1)} %bitcast.76) | data formatting | bytes 6553600 | tf_op jit(solution)/shard_map/all_to_all | solution.py:76
  366.3 43.8 %copy.106 = bf16[4,16,32,5,32,5]{4,0,5,3,2,1:T(4,128)(2,1)} copy(bf16[4,16,32,5,32,5]{1,0,5,4,3,2:T(4,128)(2,1)} %bitcast.74) | data formatting | bytes 6553600 | tf_op jit(solution)/shard_map/reshape | solution.py:43
  410.2 0.0 copy-start.11
  410.2 11.5 %fusion.72 = f32[16,32,32,32,1,1]{3,2,5,4,1,0:T(8,128)} fusion(bf16[4,16,32,5,32,5]{4,0,5,3,2,1:T(4,128)(2,1)} %copy.106, bf16[4,5,5,32]{3,0,2,1:T(4,128)(2,1)S(1)} %copy-done), kind=kOutput, calls=%fused_computation.86 | convolution fusion | flops 104857600 | bytes 5380352 | tf_op jit(solution)/shard_map/flpaqb,fabk->lkpq/dot_general | solution.py:44
  421.7 35.1 %fusion.60 = f32[2,32,32]{2,0,1:T(2,128)S(1)} fusion(f32[16,32,32,32,1,1]{3,2,5,4,1,0:T(8,128)} %fusion.72, f32[32]{0:T(128)S(1)} %copy-done.10, f32[2]{0:T(128)S(1)} %copy-done.11, s32[2,32,32]{2,0,1:T(2,128)S(1)} %copy.103, s32[2,32,32]{2,0,1:T(2,128)S(1)} %copy.102, f32[32,2]{0,1:T(2,128)S(1)} %copy-done.9), kind=kOutput, calls=%fused_computation.74 | convolution fusion | flops 13924352 | bytes 2122120 | tf_op jit(solution)/shard_map/lkpq,kc->clpq/dot_general | solution.py:46
  456.9 0.0 copy-start.4
  456.9 1.4 collective-permute-start.9
  458.3 0.0 collective-permute-start.8
  458.3 1.4 collective-permute-done.9
  459.7 2.9 collective-permute-done.8
  462.7 0.1 fusion.96
  462.7 13.6 %collective-permute-start.11 = (f32[2,56,12]{2,1,0:T(8,128)S(1)}, f32[2,56,12]{2,1,0:T(8,128)S(1)}, u32[]{:S(2)}, u32[]{:S(2)}) collective-permute-start(f32[2,56,12]{2,1,0:T(8,128)S(1)} %get-tuple-element.29), channel_id=1, source_target_pairs={{1,0},{2,1},{3,2},{4,3},{5,4},{6,5},{7,6},{64,7},{65,64},{66,65},{... | collective-permute-start | bytes 16136 | tf_op jit(solution)/shard_map/ppermute | solution.py:19
  476.4 0.0 collective-permute-start.10
  476.4 1.8 collective-permute-done.11
  478.2 5.7 %collective-permute-done.10 = f32[2,56,12]{2,1,0:T(8,128)S(1)} collective-permute-done((f32[2,56,12]{2,1,0:T(8,128)S(1)}, f32[2,56,12]{2,1,0:T(8,128)S(1)}, u32[]{:S(2)}, u32[]{:S(2)}) %collective-permute-start.10) | collective-permute-done | bytes 5408 | tf_op jit(solution)/shard_map/ppermute | solution.py:16
  483.9 0.2 convolution_bitcast_fusion
  484.1 0.8 convolution_multiply_fusion
  484.9 0.0 copy-done.4
  (21 shorter events, 0.1 us)
Async XLA Ops:
  0.6 409.5 %copy-start = (bf16[4,5,5,32]{3,0,2,1:T(4,128)(2,1)S(1)}, bf16[4,5,5,32]{3,0,2,1:T(4,128)(2,1)}, u32[]{:S(2)}) copy-start(bf16[4,5,5,32]{3,0,2,1:T(4,128)(2,1)} %param.12) | copy-start | bytes 19204
  2.1 16.5 %collective-permute-start = (f32[4,16,2,1280]{3,1,2,0:T(8,128)S(1)}, f32[4,16,2,1280]{3,1,2,0:T(8,128)S(1)}, u32[]{:S(2)}, u32[]{:S(2)}) collective-permute-start(f32[4,16,2,1280]{3,1,2,0:T(8,128)S(1)} %get-tuple-element.23), channel_id=1, source_target_pairs={{0,1},{1,2},{2,3},{3,4},{4,5},{5,6},{6,7},{7,8},{8,9},{9,10},{10,1... | collective-permute-start | bytes 1966088 | tf_op jit(solution)/shard_map/ppermute | solution.py:16
  3.8 28.0 %collective-permute-start.1 = (f32[4,16,2,1280]{3,1,2,0:T(8,128)S(1)}, f32[4,16,2,1280]{3,1,2,0:T(8,128)S(1)}, u32[]{:S(2)}, u32[]{:S(2)}) collective-permute-start(f32[4,16,2,1280]{3,1,2,0:T(8,128)S(1)} %get-tuple-element.22), channel_id=1, source_target_pairs={{1,0},{2,1},{3,2},{4,3},{5,4},{6,5},{7,6},{8,7},{9,8},{10,9},{11,1... | collective-permute-start | bytes 1966088 | tf_op jit(solution)/shard_map/ppermute | solution.py:19
  31.8 6.0 %copy-start.8 = (f32[4,16]{1,0:T(4,128)S(1)}, f32[4,16]{1,0:T(4,128)}, u32[]{:S(2)}) copy-start(f32[4,16]{1,0:T(4,128)} %param.10) | copy-start | bytes 772
  31.8 10.1 %copy-start.7 = (f32[4,16]{1,0:T(4,128)S(1)}, f32[4,16]{1,0:T(4,128)}, u32[]{:S(2)}) copy-start(f32[4,16]{1,0:T(4,128)} %param.11) | copy-start | bytes 772
  35.1 4.3 collective-permute-start.3
  37.1 4.3 collective-permute-start.2
  70.9 22.9 %copy-start.1 = (f32[4,16,20,1280]{3,1,2,0:T(8,128)}, f32[4,16,20,1280]{3,1,2,0:T(8,128)S(1)}, u32[]{:S(2)}) copy-start(f32[4,16,20,1280]{3,1,2,0:T(8,128)S(1)} %fusion.22) | copy-start | bytes 19660804
  71.0 15.4 %collective-permute-start.5 = (f32[4,16,2,1280]{3,1,2,0:T(8,128)S(1)}, f32[4,16,2,1280]{3,1,2,0:T(8,128)S(1)}, u32[]{:S(2)}, u32[]{:S(2)}) collective-permute-start(f32[4,16,2,1280]{3,1,2,0:T(8,128)S(1)} %get-tuple-element.18), channel_id=1, source_target_pairs={{1,0},{2,1},{3,2},{4,3},{5,4},{6,5},{7,6},{8,7},{9,8},{10,9},{11,1... | collective-permute-start | bytes 1966088 | tf_op jit(solution)/shard_map/ppermute | solution.py:19
  77.9 15.8 %collective-permute-start.4 = (f32[4,16,2,1280]{3,1,2,0:T(8,128)S(1)}, f32[4,16,2,1280]{3,1,2,0:T(8,128)S(1)}, u32[]{:S(2)}, u32[]{:S(2)}) collective-permute-start(f32[4,16,2,1280]{3,1,2,0:T(8,128)S(1)} %get-tuple-element.17), channel_id=1, source_target_pairs={{0,1},{1,2},{2,3},{3,4},{4,5},{5,6},{6,7},{7,8},{8,9},{9,10},{10,1... | collective-permute-start | bytes 1966088 | tf_op jit(solution)/shard_map/ppermute | solution.py:16
  86.4 26.1 %copy-start.2 = (f32[4,16,2,1280]{3,1,2,0:T(8,128)}, f32[4,16,2,1280]{3,1,2,0:T(8,128)S(1)}, u32[]{:S(2)}) copy-start(f32[4,16,2,1280]{3,1,2,0:T(8,128)S(1)} %collective-permute-done.5) | copy-start | bytes 1966084
  93.8 18.8 %copy-start.3 = (f32[4,16,2,1280]{3,1,2,0:T(8,128)}, f32[4,16,2,1280]{3,1,2,0:T(8,128)S(1)}, u32[]{:S(2)}) copy-start(f32[4,16,2,1280]{3,1,2,0:T(8,128)S(1)} %collective-permute-done.4) | copy-start | bytes 1966084
  94.5 4.3 collective-permute-start.6
  95.1 4.5 collective-permute-start.7
  212.5 6.5 %copy-start.6 = (s32[2,32,32]{2,1,0:T(8,128)S(1)}, s32[2,32,32]{2,1,0:T(8,128)}, u32[]{:S(2)}) copy-start(s32[2,32,32]{2,1,0:T(8,128)} %param.16) | copy-start | bytes 24580
  212.5 6.6 %copy-start.5 = (s32[2,32,32]{2,1,0:T(8,128)S(1)}, s32[2,32,32]{2,1,0:T(8,128)}, u32[]{:S(2)}) copy-start(s32[2,32,32]{2,1,0:T(8,128)} %param.17) | copy-start | bytes 24580
  212.5 48.8 %all-to-all-start = ((bf16[8,2,102400]{2,1,0:T(2,128)(2,1)}), bf16[8,2,102400]{2,1,0:T(2,128)(2,1)S(1)}, u32[]{:S(2)}, u32[]{:S(2)}) async-start(bf16[8,2,102400]{2,1,0:T(2,128)(2,1)} %reshape.21), calls=%async_computation | async-start | bytes 6553600 | tf_op jit(solution)/shard_map/all_to_all | solution.py:76
  410.2 11.6 %copy-start.9 = (f32[32,2]{0,1:T(2,128)S(1)}, f32[32,2]{0,1:T(2,128)}, u32[]{:S(2)}) copy-start(f32[32,2]{0,1:T(2,128)} %param.14) | copy-start | bytes 772
  410.2 11.6 %copy-start.10 = (f32[32]{0:T(128)S(1)}, f32[32]{0:T(128)}, u32[]{:S(2)}) copy-start(f32[32]{0:T(128)} %param.13) | copy-start | bytes 388
  410.2 11.6 %copy-start.11 = (f32[2]{0:T(128)S(1)}, f32[2]{0:T(128)}, u32[]{:S(2)}) copy-start(f32[2]{0:T(128)} %param.15) | copy-start | bytes 28
  456.9 28.0 %copy-start.4 = (f32[2,32,32]{2,1,0:T(8,128)}, f32[2,32,32]{2,1,0:T(8,128)S(1)}, u32[]{:S(2)}) copy-start(f32[2,32,32]{2,1,0:T(8,128)S(1)} %copy_divide_fusion) | copy-start | bytes 24580
  456.9 2.8 collective-permute-start.9
  458.3 4.4 collective-permute-start.8
  462.7 15.5 %collective-permute-start.11 = (f32[2,56,12]{2,1,0:T(8,128)S(1)}, f32[2,56,12]{2,1,0:T(8,128)S(1)}, u32[]{:S(2)}, u32[]{:S(2)}) collective-permute-start(f32[2,56,12]{2,1,0:T(8,128)S(1)} %get-tuple-element.29), channel_id=1, source_target_pairs={{1,0},{2,1},{3,2},{4,3},{5,4},{6,5},{7,6},{64,7},{65,64},{66,65},{... | collective-permute-start | bytes 16136 | tf_op jit(solution)/shard_map/ppermute | solution.py:19
  476.4 7.5 %collective-permute-start.10 = (f32[2,56,12]{2,1,0:T(8,128)S(1)}, f32[2,56,12]{2,1,0:T(8,128)S(1)}, u32[]{:S(2)}, u32[]{:S(2)}) collective-permute-start(f32[2,56,12]{2,1,0:T(8,128)S(1)} %get-tuple-element.28), channel_id=1, source_target_pairs={{0,1},{1,2},{2,3},{3,4},{4,5},{5,6},{6,7},{7,64},{64,65},{65,66},{... | collective-permute-start | bytes 16136 | tf_op jit(solution)/shard_map/ppermute | solution.py:16
where the time goes:
time: 495 us; the launch traced here: 485 us
  local copies, waits for them, and re-layouts  237 us (48%)
  waiting for transfers between devices  83.1 us (17%)
  other arithmetic  75.6 us (15%)
  matrix products  47.7 us (10%)
  starting transfers between devices  41.1 us (8%)
    unnamed x28, local copies, waits for them, and re-layouts  106 us
    all_to_all x1, local copies, waits for them, and re-layouts, on_device(): lax.all_to_all(rounded, 'gy', split_axis=3, concat_axis=2, tiled=True)  49.4 us
    reshape x1, local copies, waits for them, and re-layouts, column_probs(): fields.reshape(count_f, count_l, width_x // KERNEL, KERNEL, width_y // KE...  43.8 us
    all_to_all x1, waiting for transfers between devices, on_device(): lax.all_to_all(rounded, 'gy', split_axis=3, concat_axis=2, tiled=True)  42.2 us
    dot_general x1, matrix products, column_probs(): jnp.einsum('lkpq,kc->clpq', feats, readout, precision=lax.Precision.HIGHEST)  35.1 us
    convert_element_type x1, other arithmetic, on_device(): rounded = current.astype(jnp.bfloat16)  33.8 us
    ppermute x6, starting transfers between devices, extended_2(): lax.ppermute(lax.slice_in_dim(block, 0, width, axis=dim), axis, backward)  32.1 us
    add x1, other arithmetic, sweep(): return center + horiz * laplace + vertical * vert  29 us
  transfers between devices with their start and end apart: 13, of which 12 were waited for; matrix products, arithmetic and copies ran while one was open for 3% of the time, Pallas kernels for 0%

commit v1 on v0

v1 whole, which is shorter than its diff:
```python
import jax
import jax.numpy as jnp
from jax import lax
from jax.experimental import pallas as pl
from jax.experimental.pallas import tpu as pltpu
from jax.sharding import PartitionSpec as P

F32 = jnp.float32
BF16 = jnp.bfloat16
MESH = pl.DeviceIdType.MESH

FIELDS = 4
LEV = 16
ROWS = 20
COLS = 1280
TILE = 128
TILES = COLS // TILE
WIDE = COLS + TILE
KERNEL = 5
CHANNELS = 32
COARSE = 256
WIN = 24
HALF = WIN // 2
GY = 8
GX = 8
SLOTS = 14


def lanes(shape):
    return lax.broadcasted_iota(jnp.int32, shape, len(shape) - 1)


def sublanes(shape):
    return lax.broadcasted_iota(jnp.int32, shape, len(shape) - 2)


def stencil_row(src, coef, f, r, count, emit):
    lane = lanes((8, TILE))
    sub = sublanes((8, TILE))
    rolled = {}

    def at(row, half, t):
        return src[f, row, 8 * half : 8 * half + 8, TILE * t : TILE * t + TILE]

    def roll(half, t, shift):
        t = t % (TILES + 1)
        key = (half, t, shift)
        if key not in rolled:
            rolled[key] = pltpu.roll(at(r, half, t), shift % TILE, 1)
        return rolled[key]

    c0, c1, c2, cv = (
        [coef[f, k, 8 * half : 8 * half + 8, :] for half in range(2)] for k in range(4)
    )
    for t in range(count):
        rolled = {k: v for k, v in rolled.items() if k[1] in (t - 1, t, t + 1) or (t == 0)}
        center = [at(r, half, t) for half in range(2)]
        down = [pltpu.roll(v, 1, 0) for v in center]
        up = [pltpu.roll(v, 7, 0) for v in center]
        vert = [
            jnp.where(sub == 0, 0.0, down[0]) + jnp.where(sub == 7, up[1], up[0]),
            jnp.where(sub == 0, down[0], down[1]) + jnp.where(sub == 7, 0.0, up[1]),
        ]
        for half in range(2):
            near = (at(r - 1, half, t) + at(r + 1, half, t)) + (
                jnp.where(lane < TILE - 1, roll(half, t, -1), roll(half, t + 1, -1))
                + jnp.where(lane < 1, roll(half, t - 1, 1), roll(half, t, 1))
            )
            far = (at(r - 2, half, t) + at(r + 2, half, t)) + (
                jnp.where(lane < TILE - 2, roll(half, t, -2), roll(half, t + 1, -2))
                + jnp.where(lane < 2, roll(half, t - 1, 2), roll(half, t, 2))
            )
            emit(
                half,
                t,
                (c0[half] * center[half] + c1[half] * near)
                + (c2[half] * far + cv[half] * vert[half]),
            )


def kernel(
    state,
    h_coeff,
    v_coeff,
    weight,
    conv_bias,
    readout,
    readout_bias,
    level_base,
    level_depth,
    out,
    column_out,
    area_out,
    st,
    u,
    adv,
    ab,
    coef,
    send_x,
    recv_x,
    send_p,
    recv_p,
    send_l,
    recv_l,
    select,
    conv_l,
    dmat,
    feat,
    cf,
    frac,
    load_sem,
    store_sem,
    sx_sem,
    rx_sem,
    sp_sem,
    rp_sem,
    sl_sem,
    rl_sem,
    sf_sem,
    rf_sem,
):
    sec, gx, gy = lax.axis_index("sec"), lax.axis_index("gx"), lax.axis_index("gy")
    other = 1 - sec
    gx_low, gx_high = lax.rem(gx + GX - 1, GX), lax.rem(gx + 1, GX)
    brick = gx * GY + gy
    low, high = lax.rem(brick + GX * GY - 1, GX * GY), lax.rem(brick + 1, GX * GY)
    low_x, low_y, high_x, high_y = low // GY, lax.rem(low, GY), high // GY, lax.rem(high, GY)
    near_low, near_high = gy <= 2, gy >= 5
    near_edge = near_low | near_high
    at_end = (gy == 0) | (gy == GY - 1)

    spans = ((0, 4), (16, 4), (4, 12))
    loads = []
    for part, (first, count) in enumerate(spans):
        for f in range(FIELDS):
            copy = pltpu.make_async_copy(
                state.at[f, pl.ds(first, count)],
                st.at[f, pl.ds(first + 4, count), :, pl.ds(0, COLS)],
                load_sem.at[part, f],
            )
            copy.start()
            loads.append(copy)

    barrier = pltpu.get_barrier_semaphore()

    def hello(where):
        pl.semaphore_signal(barrier, inc=1, device_id=where, device_id_type=MESH)

    hello((sec, low_x, low_y))
    hello((sec, high_x, high_y))
    hello((other, gx, gy))
    hello((other, low_x, low_y))
    hello((other, high_x, high_y))
    for k in range(1, GY):
        hello((sec, gx, lax.rem(gy + k, GY)))
    for k in range(3):
        hello((sec, gx_high, k))
        hello((sec, gx_low, 5 + k))

    @pl.when(at_end)
    def _():
        for k in range(GY):
            hello((other, gx, k))
        for k in range(3):
            hello((other, gx_high, k))
            hello((other, gx_low, 5 + k))

    eye = (sublanes((LEV, LEV)) == lanes((LEV, LEV))).astype(F32)
    for f in range(FIELDS):
        horiz = jnp.sum(eye * h_coeff[f : f + 1, :], axis=1, keepdims=True)
        vertical = jnp.sum(eye * v_coeff[f : f + 1, :], axis=1, keepdims=True)
        for k, value in enumerate(
            (
                1.0 - 5.0 * horiz - 2.0 * vertical,
                horiz * (16.0 / 12.0),
                horiz * (-1.0 / 12.0),
                vertical,
            )
        ):
            coef[f, k] = jnp.broadcast_to(value, (LEV, TILE))

    for copy in loads[: 2 * FIELDS]:
        copy.wait()

    lane = lanes((LEV, TILE))
    group_of = lax.rem(lane + 4, TILE) // 8

    @pl.loop(0, FIELDS)
    def _(f):
        for side, first in enumerate((4, 20)):
            for row in range(4):
                send_x[side, f, row] = st[f, first + row, :, :COLS].astype(BF16)

    def edge(f, row):
        return jnp.where(lane < 64, st[f, row, :, :TILE], st[f, row, :, COLS - TILE : COLS])

    def pack(group):
        total = jnp.zeros((LEV, TILE), F32)
        for j in range(16):
            part = pltpu.roll(edge(j // 4, 4 + 4 * group + j % 4), 8 * j, 1)
            total = jnp.where(group_of == j, part, total)
        send_p[group] = total

    pack(0)
    pack(4)

    send_l[...] = jnp.zeros_like(send_l)
    for k in range(GY):
        for c in range(2):
            for kind, ref in enumerate((level_base, level_depth)):
                send_l[k, kind, 4 * c : 4 * c + 4, 0:32] = ref[c, 4 * k : 4 * k + 4, :].astype(F32)
    turn = 32 * lax.rem(gy, 4)
    for k in range(GY):
        for kind in range(2):
            send_l[k, kind] = pltpu.roll(send_l[k, kind], turn, 1)

    for copy in loads[2 * FIELDS :]:
        copy.wait()
    for group in range(1, 4):
        pack(group)

    pl.semaphore_wait(barrier, 14 + jnp.where(near_edge, 10, 0))

    def copy_x(side, f):
        where = (sec, low_x, low_y) if side == 0 else (sec, high_x, high_y)
        return pltpu.make_async_remote_copy(
            send_x.at[side, f],
            recv_x.at[1 - side, f],
            sx_sem.at[side, f],
            rx_sem.at[1 - side, f],
            device_id=where,
            device_id_type=MESH,
        )

    def copy_p(k):
        source, target, where = (
            (send_p, recv_p.at[pl.ds(1, 5)], (other, gx, gy)),
            (send_p.at[0:1], recv_p.at[pl.ds(6, 1)], (other, low_x, low_y)),
            (send_p.at[4:5], recv_p.at[pl.ds(0, 1)], (other, high_x, high_y)),
        )[k]
        return pltpu.make_async_remote_copy(
            source, target, sp_sem.at[k], rp_sem.at[k], device_id=where, device_id_type=MESH
        )

    def copy_l(k):
        to = lax.rem(gy + k, GY)
        return pltpu.make_async_remote_copy(
            send_l.at[to],
            recv_l.at[gy],
            sl_sem.at[k],
            rl_sem.at[gy],
            device_id=(sec, gx, to),
            device_id_type=MESH,
        )

    copy_p(0).start()
    copy_x(0, 0).start()
    copy_x(1, 0).start()
    copy_p(1).start()
    copy_p(2).start()
    for f in range(1, FIELDS):
        copy_x(0, f).start()
        copy_x(1, f).start()
    for k in range(1, GY):
        copy_l(k).start()
    recv_l[gy] = send_l[gy]

    row = sublanes((KERNEL * TILE, TILE))
    col = lanes((KERNEL * TILE, TILE))
    for b in range(KERNEL):
        select[:, TILE * b : TILE * b + TILE] = (row == KERNEL * col + b).astype(F32).astype(BF16)
    spread = (
        sublanes((CHANNELS * LEV, CHANNELS)) // LEV == lanes((CHANNELS * LEV, CHANNELS))
    ).astype(F32).astype(BF16)
    wide_w = lax.dot_general(
        spread, weight[...], (((1,), (1,)), ((), ())), preferred_element_type=F32
    ).astype(BF16)
    taps = KERNEL * KERNEL
    for f in range(FIELDS):
        pick = (
            sublanes((taps * FIELDS, taps * LEV))
            == (lanes((taps * FIELDS, taps * LEV)) // LEV) * FIELDS + f
        ).astype(F32).astype(BF16)
        full = jnp.dot(wide_w, pick, preferred_element_type=F32)
        shape = (CHANNELS * LEV, taps * LEV)
        same = lax.rem(sublanes(shape), LEV) == lax.rem(lanes(shape), LEV)
        conv_l[f] = jnp.where(same, full, 0.0).astype(BF16)

    for k in range(3):
        copy_p(k).wait_recv()

    @pl.loop(0, 7)
    def _(group):
        for j in range(16):
            st[j // 4, 4 * group + j % 4, :, COLS:] = pltpu.roll(
                recv_p[group], (TILE - 8 * j) % TILE, 1
            )

    def first_step(f, r):
        def emit(half, t, value):
            u[f, r - 2, 8 * half : 8 * half + 8, TILE * t : TILE * t + TILE] = value

        stencil_row(st, coef, f, r, TILES + 1, emit)

    def second_step(f, r):
        kept = {}

        def emit(half, t, value):
            adv[f, r - 2, 8 * half : 8 * half + 8, TILE * t : TILE * t + TILE] = value
            kept[half, t] = value
            if half == 1:
                both = jnp.concatenate([kept.pop((0, t)), kept.pop((1, t))], axis=0)
                ab[f, r - 2, :, TILE * t : TILE * t + TILE] = both.astype(BF16)

        stencil_row(u, coef, f, r, TILES, emit)

    def store(part, f):
        first, count = spans[part]
        return pltpu.make_async_copy(
            adv.at[f, pl.ds(first, count)], out.at[f, pl.ds(first, count)], store_sem.at[part, f]
        )

    @pl.loop(0, FIELDS)
    def _(f):
        @pl.loop(6, 22)
        def _(r):
            first_step(f, r)

        @pl.loop(6, 18)
        def _(r):
            second_step(f, r)

        store(2, f).start()

    def convolve(f, p):
        for half in range(2):
            block = ab[f, KERNEL * p : KERNEL * p + KERNEL, :, 640 * half : 640 * half + 640]
            taken = jnp.dot(
                block.reshape(KERNEL * LEV, KERNEL * TILE), select[...], preferred_element_type=F32
            ).astype(BF16)
            for a in range(KERNEL):
                for b in range(KERNEL):
                    tap = LEV * (KERNEL * a + b)
                    dmat[tap : tap + LEV, TILE * half : TILE * half + TILE] = taken[
                        LEV * a : LEV * a + LEV, TILE * b : TILE * b + TILE
                    ]
        return jnp.dot(conv_l[f], dmat[...], preferred_element_type=F32)

    for p in (1, 2):
        feat[p] = convolve(0, p)

        @pl.loop(1, FIELDS)
        def _(f):
            feat[p] += convolve(f, p)

    for p in (0, 3):
        feat[p] = jnp.zeros((CHANNELS * LEV, COARSE), F32)

    for f in range(FIELDS):
        copy_x(0, f).wait_recv()
        copy_x(1, f).wait_recv()
        for side, first in enumerate((0, 24)):
            for row in range(4):
                st[f, first + row, :, :COLS] = recv_x[side, f, row].astype(F32)

        @pl.loop(0, 4)
        def _(i):
            first_step(f, 2 + i)
            first_step(f, 22 + i)

        @pl.loop(0, 4)
        def _(i):
            second_step(f, 2 + i)
            second_step(f, 18 + i)

        store(0, f).start()
        store(1, f).start()
        for p in (0, 3):
            feat[p] += convolve(f, p)

    for k in range(1, GY):
        pltpu.make_async_remote_copy(
            send_l.at[0],
            recv_l.at[lax.rem(gy + k, GY)],
            sl_sem.at[k],
            rl_sem.at[lax.rem(gy + k, GY)],
            device_id=(sec, gx, lax.rem(gy + k, GY)),
            device_id_type=MESH,
        ).wait_recv()
    base, depth = (
        jnp.concatenate(
            [
                (recv_l[4 * t, kind] + recv_l[4 * t + 1, kind])
                + (recv_l[4 * t + 2, kind] + recv_l[4 * t + 3, kind])
                for t in range(2)
            ],
            axis=1,
        )
        for kind in range(2)
    )
    level = sublanes((LEV, COARSE)).astype(F32)
    for p in range(4):
        score = [jnp.zeros((LEV, COARSE), F32) for _ in range(2)]
        for k in range(CHANNELS):
            value = jnp.maximum(feat[p, LEV * k : LEV * k + LEV, :] + conv_bias[k], 0.0)
            for c in range(2):
                score[c] = score[c] + readout[k, c] * value
        for c in range(2):
            prob = jax.nn.sigmoid(score[c] + readout_bias[c])
            at = 4 * c + p
            least, many = base[at : at + 1, :], depth[at : at + 1, :]
            inside = (level >= least) & (level < least + many)
            total = jnp.sum(jnp.where(inside, prob, 0.0), axis=0, keepdims=True)
            cf[at : at + 1, :] = total / many

    def copy_f(index, which, slot, where):
        return pltpu.make_async_remote_copy(
            cf,
            frac.at[which, slot],
            sf_sem.at[index],
            rf_sem.at[which, slot],
            device_id=where,
            device_id_type=MESH,
        )

    home = gy + 3
    away = jnp.where(near_high, gy - 5, jnp.minimum(gy + 11, SLOTS - 1))
    away_x = jnp.where(near_high, gx_high, gx_low)

    def each_send(act):
        for k in range(1, GY):
            act(copy_f(k, 0, home, (sec, gx, lax.rem(gy + k, GY))))
        for k, y in enumerate((0, GY - 1)):
            act(copy_f(8 + k, 1, home, (other, gx, y)))

        @pl.when(near_edge)
        def _():
            for k in range(GY):
                act(copy_f(10 + k, 0, away, (sec, away_x, k)))
            for k, y in enumerate((0, GY - 1)):
                act(copy_f(18 + k, 1, away, (other, away_x, y)))

    each_send(lambda copy: copy.start())
    frac[0, home] = cf[...]
    for slot in range(SLOTS):

        @pl.when(slot != home)
        def _():
            copy_f(0, 0, slot, (sec, gx, lax.rem(gy + 1, GY))).wait_recv()

    @pl.when(at_end)
    def _():
        for slot in range(SLOTS):
            copy_f(0, 1, slot, (sec, gx, lax.rem(gy + 1, GY))).wait_recv()

    shift = lax.rem(COARSE + HALF - 32 * gy, COARSE)
    rows = SLOTS * 8
    mine = pltpu.roll(frac[0].reshape(rows, COARSE), shift, 1)[:, :TILE]
    beyond = pltpu.roll(frac[1].reshape(rows, COARSE), shift, 1)[:, :TILE]
    place = lanes((rows, TILE))
    from_other = ((place < HALF) & (gy == 0)) | ((place >= HALF + 32) & (gy == GY - 1))
    window = jnp.where(from_other, beyond, mine)
    j, i = sublanes((TILE, 32)), lanes((TILE, 32))
    band_y = ((j >= i) & (j < i + WIN)).astype(F32)
    i, m = sublanes((64, rows)), lanes((64, rows))
    which, i = i // 32, lax.rem(i, 32)
    at_row = (m // 8) * 4 + lax.rem(m, 4)
    band_x = ((lax.rem(m, 8) // 4 == which) & (at_row >= i) & (at_row < i + WIN)).astype(F32)
    sums = jnp.dot(window, band_y, precision=lax.Precision.HIGHEST, preferred_element_type=F32)
    area = jnp.dot(band_x, sums, precision=lax.Precision.HIGHEST, preferred_element_type=F32)
    area = area * (1.0 / (WIN * WIN))
    own = pltpu.roll(window, TILE - HALF, 1)
    for c in range(2):
        area_out[c] = area[32 * c : 32 * c + 32, :]
        for k in range(GY):
            at = 8 * (k + 3) + 4 * c
            column_out[c, 4 * k : 4 * k + 4, :] = own[at : at + 4, 0:32]

    for side in range(2):
        for f in range(FIELDS):
            copy_x(side, f).wait_send()
    for k in range(3):
        copy_p(k).wait_send()
    for k in range(1, GY):
        copy_l(k).wait_send()
    each_send(lambda copy: copy.wait_send())
    for part in range(3):
        for f in range(FIELDS):
            store(part, f).wait()


def on_device(
    state, h_coeff, v_coeff, conv_weight, conv_bias, readout, readout_bias, level_base, level_depth
):
    vmem = pl.BlockSpec(memory_space=pltpu.VMEM)
    smem = pl.BlockSpec(memory_space=pltpu.SMEM)
    anywhere = pl.BlockSpec(memory_space=pl.ANY)
    dma = pltpu.SemaphoreType.DMA
    taps = KERNEL * KERNEL
    out, column_fraction, area_fraction = pl.pallas_call(
        kernel,
        out_shape=(
            jax.ShapeDtypeStruct((FIELDS, ROWS, LEV, COLS), F32),
            jax.ShapeDtypeStruct((2, 32, 32), F32),
            jax.ShapeDtypeStruct((2, 32, 32), F32),
        ),
        in_specs=[anywhere, vmem, vmem, vmem, smem, smem, smem, vmem, vmem],
        out_specs=(anywhere, vmem, vmem),
        scratch_shapes=[
            pltpu.VMEM((FIELDS, ROWS + 8, LEV, WIDE), F32),
            pltpu.VMEM((FIELDS, ROWS + 4, LEV, WIDE), F32),
            pltpu.VMEM((FIELDS, ROWS, LEV, COLS), F32),
            pltpu.VMEM((FIELDS, ROWS, LEV, COLS), BF16),
            pltpu.VMEM((FIELDS, 4, LEV, TILE), F32),
            pltpu.VMEM((2, FIELDS, 4, LEV, COLS), BF16),
            pltpu.VMEM((2, FIELDS, 4, LEV, COLS), BF16),
            pltpu.VMEM((5, LEV, TILE), F32),
            pltpu.VMEM((7, LEV, TILE), F32),
            pltpu.VMEM((GY, 2, 8, TILE), F32),
            pltpu.VMEM((GY, 2, 8, TILE), F32),
            pltpu.VMEM((KERNEL * TILE, KERNEL * TILE), BF16),
            pltpu.VMEM((FIELDS, CHANNELS * LEV, taps * LEV), BF16),
            pltpu.VMEM((taps * LEV, COARSE), BF16),
            pltpu.VMEM((4, CHANNELS * LEV, COARSE), F32),
            pltpu.VMEM((8, COARSE), F32),
            pltpu.VMEM((2, SLOTS, 8, COARSE), F32),
            dma((3, FIELDS)),
            dma((3, FIELDS)),
            dma((2, FIELDS)),
            dma((2, FIELDS)),
            dma((3,)),
            dma((3,)),
            dma((GY,)),
            dma((GY,)),
            dma((20,)),
            dma((2, SLOTS)),
        ],
        compiler_params=pltpu.CompilerParams(
            collective_id=0, has_side_effects=True, vmem_limit_bytes=56 * 2**20
        ),
        name="steps_and_fractions",
    )(
        jnp.transpose(state, (0, 2, 1, 3)),
        h_coeff,
        v_coeff,
        jnp.transpose(conv_weight, (1, 2, 0, 3)).reshape(taps * FIELDS, CHANNELS),
        conv_bias,
        readout,
        readout_bias,
        level_base,
        level_depth,
    )
    return jnp.transpose(out, (0, 2, 1, 3)), column_fraction, area_fraction


def solution(mesh):
    in_specs = (
        P(None, None, ("gx", "gy"), "sec"),
        P(),
        P(),
        P(),
        P(),
        P(),
        P(),
        P(None, "gx", ("sec", "gy")),
        P(None, "gx", ("sec", "gy")),
    )
    out_specs = (
        P(None, None, ("gx", "gy"), "sec"),
        P(None, "gx", ("sec", "gy")),
        P(None, "gx", ("sec", "gy")),
    )
    return jax.shard_map(
        on_device, mesh=mesh, in_specs=in_specs, out_specs=out_specs, check_vma=False
    )
```

time: 495 us -> 84.8 us (0.17); the launches traced: 485 us -> 84.5 us
  local copies, waits for them, and re-layouts: 237 us -> 10.1 us
  waiting for transfers between devices: 83.1 us -> 0 us
  other arithmetic: 75.6 us -> 0 us
  Pallas kernels: 0 us -> 73.8 us
  matrix products: 47.7 us -> 0 us
  starting transfers between devices: 41.1 us -> 0 us
    unnamed x28 -> x8, local copies, waits for them, and re-layouts: 106 us -> 8.69 us
    pallas_call x0 -> x1, Pallas kernels: none -> 73.8 us  [on_device(): pl.pallas_call(kernel, out_shape=(jax.ShapeDtypeStruct((FIELDS, ROWS, LEV...]
    all_to_all x1 -> x0, local copies, waits for them, and re-layouts: 49.4 us -> none  [on_device(): lax.all_to_all(rounded, 'gy', split_axis=3, concat_axis=2, tiled=True)]
    dot_general x4 -> x0, matrix products: 47.7 us -> none  [the longest x1 35.1 us: column_probs(): jnp.einsum('lkpq,kc->clpq', feats, readout, precision=lax.Precision.HIGHEST)]
    reshape x1, local copies, waits for them, and re-layouts: 43.8 us -> 1.37 us  [on_device(): jnp.transpose(conv_weight, (1, 2, 0, 3)).reshape(taps * FIELDS, CHANNELS)]
    all_to_all x1 -> x0, waiting for transfers between devices: 42.2 us -> none  [on_device(): lax.all_to_all(rounded, 'gy', split_axis=3, concat_axis=2, tiled=True)]
    ppermute x12 -> x0, waiting for transfers between devices: 40.9 us -> none  [the longest x6 27.2 us: extended_2(): lax.ppermute(lax.slice_in_dim(block, block.shape[dim] - width, None, axis...]
    ppermute x12 -> x0, starting transfers between devices: 34.6 us -> none  [the longest x6 32.1 us: extended_2(): lax.ppermute(lax.slice_in_dim(block, 0, width, axis=dim), axis, backward)]
  transfers between devices with their start and end apart: 13 -> 0, of which waited for: 12 -> 0; matrix products, arithmetic and copies ran while one was open for 3% -> 0% of each run, Pallas kernels for 0% -> 0%
where the time goes in v1:
time: 84.8 us; the launch traced here: 84.5 us
  Pallas kernels  73.8 us (87%)
  local copies, waits for them, and re-layouts  10.1 us (12%)
    pallas_call x1, Pallas kernels, on_device(): pl.pallas_call(kernel, out_shape=(jax.ShapeDtypeStruct((FIELDS, ROWS, LEV...  73.8 us
    unnamed x8, local copies, waits for them, and re-layouts  8.69 us

profile of v1, /device:TPU:0, one launch (start us, length us, event | category | flops | bytes accessed | tf_op | source)
XLA Modules:
  0.0 84.5 jit_solution(372797137897974420)
XLA Ops:
  0.6 1.4 %copy.13.readout = f32[32,2]{1,0:T(8,128)} copy(f32[32,2]{0,1:T(2,128)} %param.14) | data formatting | bytes 512 | tf_op args[5]
  2.0 1.4 %reshape.9.weight = bf16[100,32]{1,0:T(8,128)(2,1)} reshape(bf16[5,5,4,32]{3,2,1,0:T(4,128)(2,1)} %bitcast.5) | data formatting | bytes 12800 | tf_op jit(solution)/shard_map/reshape | solution.py:546
  3.4 73.8 %steps_and_fractions.1 = (f32[4,20,16,1280]{3,2,1,0:T(8,128)}, f32[2,32,32]{2,1,0:T(8,128)}, f32[2,32,32]{2,1,0:T(8,128)}) custom-call(f32[4,20,16,1280]{3,2,1,0:T(8,128)} %bitcast.3, f32[4,16]{1,0:T(4,128)} %h_coeff.1, f32[4,16]{1,0:T(4,128)} %v_coeff.1, bf16[100,32]{1,0:T(8,128)(2,1)} %reshape.9.weight, f32[32]{0:T(128)} %conv_bias.1, ...), custom_call_target="tpu_custom_call" | custom-call | tf_op jit(solution)/shard_map/steps_and_fractions/pallas_call | solution.py:500
  77.2 0.0 copy-start.1
  77.2 0.0 copy-start
  77.2 6.1 %copy.17 = f32[4,16,20,1280]{3,1,2,0:T(8,128)} copy(f32[4,16,20,1280]{3,1,2,0:T(8,128)} %bitcast.4) | data formatting | bytes 13107200
  83.3 0.0 copy-done.1
  83.3 0.6 copy.18
  83.9 0.0 copy-done
  83.9 0.6 copy.19
Async XLA Ops:
  77.2 6.1 %copy-start.1 = (f32[2,32,32]{2,1,0:T(8,128)S(1)}, f32[2,32,32]{2,1,0:T(8,128)}, u32[]{:S(2)}) copy-start(f32[2,32,32]{2,1,0:T(8,128)} %get-tuple-element.13) | copy-start | bytes 24580
  77.2 6.7 %copy-start = (f32[2,32,32]{2,1,0:T(8,128)S(1)}, f32[2,32,32]{2,1,0:T(8,128)}, u32[]{:S(2)}) copy-start(f32[2,32,32]{2,1,0:T(8,128)} %get-tuple-element.14) | copy-start | bytes 24580

commit v2 on v1

--- a/solution.py
+++ b/solution.py
@@ -34,48 +34,45 @@
     return lax.broadcasted_iota(jnp.int32, shape, len(shape) - 2)
 
 
-def stencil_row(src, coef, f, r, count, emit):
-    lane = lanes((8, TILE))
+def stencil(src, coef, band, f, rows, count, emit):
+    lane = lanes((LEV, TILE))
     sub = sublanes((8, TILE))
-    rolled = {}
-
-    def at(row, half, t):
-        return src[f, row, 8 * half : 8 * half + 8, TILE * t : TILE * t + TILE]
-
-    def roll(half, t, shift):
-        t = t % (TILES + 1)
-        key = (half, t, shift)
-        if key not in rolled:
-            rolled[key] = pltpu.roll(at(r, half, t), shift % TILE, 1)
-        return rolled[key]
-
-    c0, c1, c2, cv = (
-        [coef[f, k, 8 * half : 8 * half + 8, :] for half in range(2)] for k in range(4)
-    )
-    for t in range(count):
-        rolled = {k: v for k, v in rolled.items() if k[1] in (t - 1, t, t + 1) or (t == 0)}
-        center = [at(r, half, t) for half in range(2)]
-        down = [pltpu.roll(v, 1, 0) for v in center]
-        up = [pltpu.roll(v, 7, 0) for v in center]
-        vert = [
-            jnp.where(sub == 0, 0.0, down[0]) + jnp.where(sub == 7, up[1], up[0]),
-            jnp.where(sub == 0, down[0], down[1]) + jnp.where(sub == 7, 0.0, up[1]),
-        ]
-        for half in range(2):
-            near = (at(r - 1, half, t) + at(r + 1, half, t)) + (
-                jnp.where(lane < TILE - 1, roll(half, t, -1), roll(half, t + 1, -1))
-                + jnp.where(lane < 1, roll(half, t - 1, 1), roll(half, t, 1))
+    tiles = TILES + 1
+
+    def at(r, t):
+        return src[f, r, :, TILE * t : TILE * t + TILE]
+
+    parts = []
+    for r in rows:
+        for t in range(tiles):
+            value = at(r, t)
+            head = value.astype(BF16)
+            tail = (value - head.astype(F32)).astype(BF16)
+            parts.append(jnp.concatenate([head, tail], axis=1))
+    sums = jnp.dot(jnp.concatenate(parts, axis=0), band[...], preferred_element_type=F32)
+
+    c0, c1, c2 = coef[f, 0], coef[f, 1], coef[f, 2]
+    for q, r in enumerate(rows):
+
+        def along_y(t, part):
+            first = LEV * (q * tiles + t % tiles)
+            return sums[first : first + LEV, TILE * part : TILE * part + TILE]
+
+        for t in range(count):
+            value = at(r, t)
+            y = along_y(t, 0) + jnp.where(lane < 64, along_y(t - 1, 1), along_y(t + 1, 1))
+            low, high = value[:8], value[8:]
+            low_down, high_down = pltpu.roll(low, 1, 0), pltpu.roll(high, 1, 0)
+            low_up, high_up = pltpu.roll(low, 7, 0), pltpu.roll(high, 7, 0)
+            vert = jnp.concatenate(
+                [
+                    jnp.where(sub == 0, 0.0, low_down) + jnp.where(sub == 7, high_up, low_up),
+                    jnp.where(sub == 0, low_down, high_down) + jnp.where(sub == 7, 0.0, high_up),
+                ],
+                axis=0,
             )
-            far = (at(r - 2, half, t) + at(r + 2, half, t)) + (
-                jnp.where(lane < TILE - 2, roll(half, t, -2), roll(half, t + 1, -2))
-                + jnp.where(lane < 2, roll(half, t - 1, 2), roll(half, t, 2))
-            )
-            emit(
-                half,
-                t,
-                (c0[half] * center[half] + c1[half] * near)
-                + (c2[half] * far + cv[half] * vert[half]),
-            )
+            x = 16.0 * (at(r - 1, t) + at(r + 1, t)) - (at(r - 2, t) + at(r + 2, t))
+            emit(r, t, (c0 * value + c1 * (x + y)) + c2 * vert)
 
 
 def kernel(
@@ -88,14 +85,14 @@
     readout_bias,
     level_base,
     level_depth,
-    out,
+    adv,
     column_out,
     area_out,
     st,
     u,
-    adv,
     ab,
     coef,
+    band,
     send_x,
     recv_x,
     send_p,
@@ -103,13 +100,13 @@
     send_l,
     recv_l,
     select,
+    taps_w,
     conv_l,
     dmat,
     feat,
     cf,
     frac,
     load_sem,
-    store_sem,
     sx_sem,
     rx_sem,
     sp_sem,
@@ -172,12 +169,17 @@
         for k, value in enumerate(
             (
                 1.0 - 5.0 * horiz - 2.0 * vertical,
-                horiz * (16.0 / 12.0),
-                horiz * (-1.0 / 12.0),
+                horiz * (1.0 / 12.0),
                 vertical,
             )
         ):
             coef[f, k] = jnp.broadcast_to(value, (LEV, TILE))
+
+    i, j = sublanes((2 * TILE, 2 * TILE)), lanes((2 * TILE, 2 * TILE))
+    away = jnp.abs(lax.rem(i, TILE) - lax.rem(j, TILE))
+    away = jnp.where(j < TILE, away, TILE - away)
+    taps_y = jnp.where(away == 1, 16.0, jnp.where(away == 2, -1.0, 0.0))
+    band[...] = taps_y.astype(BF16)
 
     for copy in loads[: 2 * FIELDS]:
         copy.wait()
@@ -203,16 +205,6 @@
 
     pack(0)
     pack(4)
-
-    send_l[...] = jnp.zeros_like(send_l)
-    for k in range(GY):
-        for c in range(2):
-            for kind, ref in enumerate((level_base, level_depth)):
-                send_l[k, kind, 4 * c : 4 * c + 4, 0:32] = ref[c, 4 * k : 4 * k + 4, :].astype(F32)
-    turn = 32 * lax.rem(gy, 4)
-    for k in range(GY):
-        for kind in range(2):
-            send_l[k, kind] = pltpu.roll(send_l[k, kind], turn, 1)
 
     for copy in loads[2 * FIELDS :]:
         copy.wait()
@@ -253,14 +245,21 @@
             device_id_type=MESH,
         )
 
-    copy_p(0).start()
-    copy_x(0, 0).start()
-    copy_x(1, 0).start()
-    copy_p(1).start()
-    copy_p(2).start()
-    for f in range(1, FIELDS):
+    for k in range(3):
+        copy_p(k).start()
+    for f in range(FIELDS):
         copy_x(0, f).start()
         copy_x(1, f).start()
+
+    send_l[...] = jnp.zeros_like(send_l)
+    for k in range(GY):
+        for c in range(2):
+            for kind, ref in enumerate((level_base, level_depth)):
+                send_l[k, kind, 4 * c : 4 * c + 4, 0:32] = ref[c, 4 * k : 4 * k + 4, :].astype(F32)
+    turn = 32 * lax.rem(gy, 4)
+    for k in range(GY):
+        for kind in range(2):
+            send_l[k, kind] = pltpu.roll(send_l[k, kind], turn, 1)
     for k in range(1, GY):
         copy_l(k).start()
     recv_l[gy] = send_l[gy]
@@ -269,93 +268,84 @@
     col = lanes((KERNEL * TILE, TILE))
     for b in range(KERNEL):
         select[:, TILE * b : TILE * b + TILE] = (row == KERNEL * col + b).astype(F32).astype(BF16)
-    spread = (
-        sublanes((CHANNELS * LEV, CHANNELS)) // LEV == lanes((CHANNELS * LEV, CHANNELS))
-    ).astype(F32).astype(BF16)
+    taps = KERNEL * KERNEL
+    for tap in range(taps):
+        taps_w[FIELDS * tap : FIELDS * tap + FIELDS, :] = weight[tap // KERNEL, tap % KERNEL].astype(F32)
+    shape = (CHANNELS * LEV, CHANNELS)
+    spread = (sublanes(shape) // LEV == lanes(shape)).astype(F32).astype(BF16)
     wide_w = lax.dot_general(
-        spread, weight[...], (((1,), (1,)), ((), ())), preferred_element_type=F32
+        spread,
+        taps_w[...].astype(BF16),
+        (((1,), (1,)), ((), ())),
+        preferred_element_type=F32,
     ).astype(BF16)
-    taps = KERNEL * KERNEL
-    for f in range(FIELDS):
-        pick = (
-            sublanes((taps * FIELDS, taps * LEV))
-            == (lanes((taps * FIELDS, taps * LEV)) // LEV) * FIELDS + f
-        ).astype(F32).astype(BF16)
-        full = jnp.dot(wide_w, pick, preferred_element_type=F32)
-        shape = (CHANNELS * LEV, taps * LEV)
-        same = lax.rem(sublanes(shape), LEV) == lax.rem(lanes(shape), LEV)
-        conv_l[f] = jnp.where(same, full, 0.0).astype(BF16)
-
-    for k in range(3):
-        copy_p(k).wait_recv()
-
-    @pl.loop(0, 7)
-    def _(group):
+    shape = (taps * FIELDS, FIELDS * taps * LEV)
+    tap_at = lanes(shape) // LEV
+    pick = (sublanes(shape) == lax.rem(tap_at, taps) * FIELDS + tap_at // taps).astype(F32)
+    full = jnp.dot(wide_w, pick.astype(BF16), preferred_element_type=F32)
+    same = lax.rem(sublanes(full.shape), LEV) == lax.rem(lanes(full.shape), LEV)
+    conv_l[...] = jnp.where(same, full, 0.0).astype(BF16)
+
+    def unpack(group):
         for j in range(16):
             st[j // 4, 4 * group + j % 4, :, COLS:] = pltpu.roll(
                 recv_p[group], (TILE - 8 * j) % TILE, 1
             )
 
-    def first_step(f, r):
-        def emit(half, t, value):
-            u[f, r - 2, 8 * half : 8 * half + 8, TILE * t : TILE * t + TILE] = value
-
-        stencil_row(st, coef, f, r, TILES + 1, emit)
-
-    def second_step(f, r):
-        kept = {}
-
-        def emit(half, t, value):
-            adv[f, r - 2, 8 * half : 8 * half + 8, TILE * t : TILE * t + TILE] = value
-            kept[half, t] = value
-            if half == 1:
-                both = jnp.concatenate([kept.pop((0, t)), kept.pop((1, t))], axis=0)
-                ab[f, r - 2, :, TILE * t : TILE * t + TILE] = both.astype(BF16)
-
-        stencil_row(u, coef, f, r, TILES, emit)
-
-    def store(part, f):
-        first, count = spans[part]
-        return pltpu.make_async_copy(
-            adv.at[f, pl.ds(first, count)], out.at[f, pl.ds(first, count)], store_sem.at[part, f]
-        )
+    copy_p(0).wait_recv()
+    for group in range(1, 6):
+        unpack(group)
+
+    def first_step(f, rows):
+        def emit(r, t, value):
+            u[f, r - 2, :, TILE * t : TILE * t + TILE] = value
+
+        stencil(st, coef, band, f, rows, TILES + 1, emit)
+
+    def second_step(f, rows):
+        def emit(r, t, value):
+            adv[f, r - 2, :, TILE * t : TILE * t + TILE] = value
+            ab[f, r - 2, :, TILE * t : TILE * t + TILE] = value.astype(BF16)
+
+        stencil(u, coef, band, f, rows, TILES, emit)
 
     @pl.loop(0, FIELDS)
     def _(f):
-        @pl.loop(6, 22)
-        def _(r):
-            first_step(f, r)
-
-        @pl.loop(6, 18)
-        def _(r):
-            second_step(f, r)
-
-        store(2, f).start()
-
-    def convolve(f, p):
-        for half in range(2):
-            block = ab[f, KERNEL * p : KERNEL * p + KERNEL, :, 640 * half : 640 * half + 640]
-            taken = jnp.dot(
-                block.reshape(KERNEL * LEV, KERNEL * TILE), select[...], preferred_element_type=F32
-            ).astype(BF16)
-            for a in range(KERNEL):
-                for b in range(KERNEL):
-                    tap = LEV * (KERNEL * a + b)
-                    dmat[tap : tap + LEV, TILE * half : TILE * half + TILE] = taken[
-                        LEV * a : LEV * a + LEV, TILE * b : TILE * b + TILE
-                    ]
-        return jnp.dot(conv_l[f], dmat[...], preferred_element_type=F32)
-
-    for p in (1, 2):
-        feat[p] = convolve(0, p)
-
-        @pl.loop(1, FIELDS)
-        def _(f):
-            feat[p] += convolve(f, p)
-
-    for p in (0, 3):
-        feat[p] = jnp.zeros((CHANNELS * LEV, COARSE), F32)
-
+        first_step(f, range(6, 14))
+        first_step(f, range(14, 22))
+        second_step(f, range(6, 18))
+
+    def take(f, pair, slot):
+        blocks = [
+            ab[f, KERNEL * p : KERNEL * p + KERNEL, :, 640 * half : 640 * half + 640].reshape(
+                KERNEL * LEV, KERNEL * TILE
+            )
+            for p in pair
+            for half in range(2)
+        ]
+        taken = jnp.dot(
+            jnp.concatenate(blocks, axis=0), select[...], preferred_element_type=F32
+        ).astype(BF16)
+        for i in range(2):
+            for half in range(2):
+                for a in range(KERNEL):
+                    first = LEV * (KERNEL * (2 * i + half) + a)
+                    for b in range(KERNEL):
+                        tap = LEV * (taps * f + KERNEL * a + b)
+                        dmat[slot, i, tap : tap + LEV, TILE * half : TILE * half + TILE] = taken[
+                            first : first + LEV, TILE * b : TILE * b + TILE
+                        ]
+
+    for f in range(FIELDS):
+        take(f, (1, 2), 0)
+    for i, p in enumerate((1, 2)):
+        feat[p] = jnp.dot(conv_l[...], dmat[0, i], preferred_element_type=F32)
+
+    for k in range(1, 3):
+        copy_p(k).wait_recv()
+    unpack(0)
+    unpack(6)
+    early = 9 * TILE
     for f in range(FIELDS):
         copy_x(0, f).wait_recv()
         copy_x(1, f).wait_recv()
@@ -363,20 +353,16 @@
             for row in range(4):
                 st[f, first + row, :, :COLS] = recv_x[side, f, row].astype(F32)
 
-        @pl.loop(0, 4)
-        def _(i):
-            first_step(f, 2 + i)
-            first_step(f, 22 + i)
-
-        @pl.loop(0, 4)
-        def _(i):
-            second_step(f, 2 + i)
-            second_step(f, 18 + i)
-
-        store(0, f).start()
-        store(1, f).start()
-        for p in (0, 3):
-            feat[p] += convolve(f, p)
+        first_step(f, (2, 3, 4, 5, 22, 23, 24, 25))
+        second_step(f, (2, 3, 4, 5, 18, 19, 20, 21))
+        take(f, (0, 3), 1)
+        if f == 2:
+            for i, p in enumerate((0, 3)):
+                feat[p] = jnp.dot(
+                    conv_l[:, :early], dmat[1, i, :early], preferred_element_type=F32
+                )
+    for i, p in enumerate((0, 3)):
+        feat[p] += jnp.dot(conv_l[:, early:], dmat[1, i, early:], preferred_element_type=F32)
 
     for k in range(1, GY):
         pltpu.make_async_remote_copy(
@@ -404,7 +390,7 @@
         for k in range(CHANNELS):
             value = jnp.maximum(feat[p, LEV * k : LEV * k + LEV, :] + conv_bias[k], 0.0)
             for c in range(2):
-                score[c] = score[c] + readout[k, c] * value
+                score[c] = score[c] + readout[c, k] * value
         for c in range(2):
             prob = jax.nn.sigmoid(score[c] + readout_bias[c])
             at = 4 * c + p
@@ -484,9 +470,19 @@
     for k in range(1, GY):
         copy_l(k).wait_send()
     each_send(lambda copy: copy.wait_send())
-    for part in range(3):
-        for f in range(FIELDS):
-            store(part, f).wait()
+
+
+def write_out(adv, column_fraction, area_fraction, out, column_out, area_out, sem):
+    copies = [
+        pltpu.make_async_copy(adv.at[f], out.at[f], sem.at[f]) for f in range(FIELDS)
+    ] + [
+        pltpu.make_async_copy(column_fraction, column_out, sem.at[FIELDS]),
+        pltpu.make_async_copy(area_fraction, area_out, sem.at[FIELDS + 1]),
+    ]
+    for copy in copies:
+        copy.start()
+    for copy in copies:
+        copy.wait()
 
 
 def on_device(
@@ -500,18 +496,18 @@
     out, column_fraction, area_fraction = pl.pallas_call(
         kernel,
         out_shape=(
-            jax.ShapeDtypeStruct((FIELDS, ROWS, LEV, COLS), F32),
-            jax.ShapeDtypeStruct((2, 32, 32), F32),
-            jax.ShapeDtypeStruct((2, 32, 32), F32),
+            pltpu.VMEM((FIELDS, ROWS, LEV, COLS), F32),
+            pltpu.VMEM((2, 32, 32), F32),
+            pltpu.VMEM((2, 32, 32), F32),
         ),
         in_specs=[anywhere, vmem, vmem, vmem, smem, smem, smem, vmem, vmem],
-        out_specs=(anywhere, vmem, vmem),
+        out_specs=(vmem, vmem, vmem),
         scratch_shapes=[
             pltpu.VMEM((FIELDS, ROWS + 8, LEV, WIDE), F32),
             pltpu.VMEM((FIELDS, ROWS + 4, LEV, WIDE), F32),
-            pltpu.VMEM((FIELDS, ROWS, LEV, COLS), F32),
             pltpu.VMEM((FIELDS, ROWS, LEV, COLS), BF16),
-            pltpu.VMEM((FIELDS, 4, LEV, TILE), F32),
+            pltpu.VMEM((FIELDS, 3, LEV, TILE), F32),
+            pltpu.VMEM((2 * TILE, 2 * TILE), BF16),
             pltpu.VMEM((2, FIELDS, 4, LEV, COLS), BF16),
             pltpu.VMEM((2, FIELDS, 4, LEV, COLS), BF16),
             pltpu.VMEM((5, LEV, TILE), F32),
@@ -519,12 +515,12 @@
             pltpu.VMEM((GY, 2, 8, TILE), F32),
             pltpu.VMEM((GY, 2, 8, TILE), F32),
             pltpu.VMEM((KERNEL * TILE, KERNEL * TILE), BF16),
-            pltpu.VMEM((FIELDS, CHANNELS * LEV, taps * LEV), BF16),
-            pltpu.VMEM((taps * LEV, COARSE), BF16),
+            pltpu.VMEM((taps * FIELDS, CHANNELS), F32),
+            pltpu.VMEM((CHANNELS * LEV, FIELDS * taps * LEV), BF16),
+            pltpu.VMEM((2, 2, FIELDS * taps * LEV, COARSE), BF16),
             pltpu.VMEM((4, CHANNELS * LEV, COARSE), F32),
             pltpu.VMEM((8, COARSE), F32),
             pltpu.VMEM((2, SLOTS, 8, COARSE), F32),
-            dma((3, FIELDS)),
             dma((3, FIELDS)),
             dma((2, FIELDS)),
             dma((2, FIELDS)),
@@ -536,20 +532,33 @@
             dma((2, SLOTS)),
         ],
         compiler_params=pltpu.CompilerParams(
-            collective_id=0, has_side_effects=True, vmem_limit_bytes=56 * 2**20
+            collective_id=0, has_side_effects=True, vmem_limit_bytes=48 * 2**20
         ),
         name="steps_and_fractions",
     )(
         jnp.transpose(state, (0, 2, 1, 3)),
         h_coeff,
         v_coeff,
-        jnp.transpose(conv_weight, (1, 2, 0, 3)).reshape(taps * FIELDS, CHANNELS),
+        jnp.transpose(conv_weight, (1, 2, 0, 3)),
         conv_bias,
-        readout,
+        jnp.transpose(readout),
         readout_bias,
         level_base,
         level_depth,
     )
+    out, column_fraction, area_fraction = pl.pallas_call(
+        write_out,
+        out_shape=(
+            jax.ShapeDtypeStruct((FIELDS, ROWS, LEV, COLS), F32),
+            jax.ShapeDtypeStruct((2, 32, 32), F32),
+            jax.ShapeDtypeStruct((2, 32, 32), F32),
+        ),
+        in_specs=[vmem, vmem, vmem],
+        out_specs=(anywhere, anywhere, anywhere),
+        scratch_shapes=[dma((FIELDS + 2,))],
+        compiler_params=pltpu.CompilerParams(vmem_limit_bytes=2**20),
+        name="write_out",
+    )(out, column_fraction, area_fraction)
     return jnp.transpose(out, (0, 2, 1, 3)), column_fraction, area_fraction
 
 

time: 84.8 us -> 54.4 us (0.64)
  Pallas kernels: 73.8 us -> 53.6 us
  local copies, waits for them, and re-layouts: 10.1 us -> 0 us
    pallas_call x1 -> x2, Pallas kernels: 73.8 us -> 53.6 us  [the longest x1 50.7 us: on_device(): pl.pallas_call(kernel, out_shape=(pltpu.VMEM((FIELDS, ROWS, LEV, COLS), F...]
    unnamed x8 -> x0, local copies, waits for them, and re-layouts: 8.69 us -> none
    reshape x1 -> x0, local copies, waits for them, and re-layouts: 1.37 us -> none  [on_device(): jnp.transpose(conv_weight, (1, 2, 0, 3)).reshape(taps * FIELDS, CHANNELS)]
where the time goes in v2:
time: 54.4 us; the launch traced here: 54.2 us
  Pallas kernels  53.6 us (99%)
  between operations  0.64 us (1%)
    pallas_call x1, Pallas kernels, on_device(): pl.pallas_call(kernel, out_shape=(pltpu.VMEM((FIELDS, ROWS, LEV, COLS), F...  50.7 us
    pallas_call x1, Pallas kernels, on_device(): pl.pallas_call(write_out, out_shape=(jax.ShapeDtypeStruct((FIELDS, ROWS,...  2.84 us

profile of v2, /device:TPU:0, one launch (start us, length us, event | category | flops | bytes accessed | tf_op | source)
XLA Modules:
  0.0 54.2 jit_solution(7809967988700559582)
XLA Ops:
  0.6 50.7 %steps_and_fractions.1 = (f32[4,20,16,1280]{3,2,1,0:T(8,128)S(1)}, f32[2,32,32]{2,1,0:T(8,128)S(1)}, f32[2,32,32]{2,1,0:T(8,128)S(1)}) custom-call(f32[4,20,16,1280]{3,2,1,0:T(8,128)} %bitcast.4, f32[4,16]{1,0:T(4,128)} %h_coeff.1, f32[4,16]{1,0:T(4,128)} %v_coeff.1, bf16[5,5,4,32]{3,2,1,0:T(4,128)(2,1)} %bitcast.5, f32[32]{0:T(128)} %conv_bias.1, ...), custom_call_target="tpu_custom_call" | custom-call | tf_op jit(solution)/shard_map/steps_and_fractions/pallas_call | solution.py:496
  51.4 2.8 %write_out.1 = (f32[4,20,16,1280]{3,2,1,0:T(8,128)}, f32[2,32,32]{2,1,0:T(8,128)}, f32[2,32,32]{2,1,0:T(8,128)}) custom-call(f32[4,20,16,1280]{3,2,1,0:T(8,128)S(1)} %get-tuple-element.9.adv, f32[2,32,32]{2,1,0:T(8,128)S(1)} %get-tuple-element.10.column_fraction, f32[2,32,32]{2,1,0:T(8,128)S(1)} %get-tuple-element.11.area_fraction), custom_call_target="tpu_custom_call" | custom-call | tf_op jit(solution)/shard_map/write_out/pallas_call | solution.py:549

commit v3 on v2

--- a/solution.py
+++ b/solution.py
@@ -34,17 +34,18 @@
     return lax.broadcasted_iota(jnp.int32, shape, len(shape) - 2)
 
 
-def stencil(src, coef, band, f, rows, count, emit):
+def stencil(src, coef, band, f, rows, wanted, emit):
     lane = lanes((LEV, TILE))
     sub = sublanes((8, TILE))
     tiles = TILES + 1
+    needed = sorted({(t + d) % tiles for t in wanted for d in (-1, 0, 1)})
 
     def at(r, t):
         return src[f, r, :, TILE * t : TILE * t + TILE]
 
     parts = []
     for r in rows:
-        for t in range(tiles):
+        for t in needed:
             value = at(r, t)
             head = value.astype(BF16)
             tail = (value - head.astype(F32)).astype(BF16)
@@ -55,10 +56,10 @@
     for q, r in enumerate(rows):
 
         def along_y(t, part):
-            first = LEV * (q * tiles + t % tiles)
+            first = LEV * (q * len(needed) + needed.index(t % tiles))
             return sums[first : first + LEV, TILE * part : TILE * part + TILE]
 
-        for t in range(count):
+        for t in wanted:
             value = at(r, t)
             y = along_y(t, 0) + jnp.where(lane < 64, along_y(t - 1, 1), along_y(t + 1, 1))
             low, high = value[:8], value[8:]
@@ -162,6 +163,74 @@
             hello((other, gx_high, k))
             hello((other, gx_low, 5 + k))
 
+    for copy in loads[: 2 * FIELDS]:
+        copy.wait()
+
+    lane = lanes((LEV, TILE))
+    group_of = lax.rem(lane + 4, TILE) // 8
+
+    @pl.loop(0, FIELDS)
+    def _(f):
+        for side, first in enumerate((4, 20)):
+            for row in range(4):
+                send_x[side, f, row] = st[f, first + row, :, :COLS].astype(BF16)
+
+    pl.semaphore_wait(barrier, 14 + jnp.where(near_edge, 10, 0))
+
+    def copy_x(side, f):
+        where = (sec, low_x, low_y) if side == 0 else (sec, high_x, high_y)
+        return pltpu.make_async_remote_copy(
+            send_x.at[side, f],
+            recv_x.at[1 - side, f],
+            sx_sem.at[side, f],
+            rx_sem.at[1 - side, f],
+            device_id=where,
+            device_id_type=MESH,
+        )
+
+    def copy_p(k):
+        source, target, where = (
+            (send_p, recv_p.at[pl.ds(1, 5)], (other, gx, gy)),
+            (send_p.at[0:1], recv_p.at[pl.ds(6, 1)], (other, low_x, low_y)),
+            (send_p.at[4:5], recv_p.at[pl.ds(0, 1)], (other, high_x, high_y)),
+        )[k]
+        return pltpu.make_async_remote_copy(
+            source, target, sp_sem.at[k], rp_sem.at[k], device_id=where, device_id_type=MESH
+        )
+
+    def copy_l(k):
+        to = lax.rem(gy + k, GY)
+        return pltpu.make_async_remote_copy(
+            send_l.at[to],
+            recv_l.at[gy],
+            sl_sem.at[k],
+            rl_sem.at[gy],
+            device_id=(sec, gx, to),
+            device_id_type=MESH,
+        )
+
+    for f in range(FIELDS):
+        copy_x(0, f).start()
+        copy_x(1, f).start()
+
+    def edge(f, row):
+        return jnp.where(lane < 64, st[f, row, :, :TILE], st[f, row, :, COLS - TILE : COLS])
+
+    def pack(group):
+        total = jnp.zeros((LEV, TILE), F32)
+        for j in range(16):
+            part = pltpu.roll(edge(j // 4, 4 + 4 * group + j % 4), 8 * j, 1)
+            total = jnp.where(group_of == j, part, total)
+        send_p[group] = total
+
+    for copy in loads[2 * FIELDS :]:
+        copy.wait()
+    for group in range(5):
+        pack(group)
+
+    for k in range(3):
+        copy_p(k).start()
+
     eye = (sublanes((LEV, LEV)) == lanes((LEV, LEV))).astype(F32)
     for f in range(FIELDS):
         horiz = jnp.sum(eye * h_coeff[f : f + 1, :], axis=1, keepdims=True)
@@ -181,75 +250,6 @@
     taps_y = jnp.where(away == 1, 16.0, jnp.where(away == 2, -1.0, 0.0))
     band[...] = taps_y.astype(BF16)
 
-    for copy in loads[: 2 * FIELDS]:
-        copy.wait()
-
-    lane = lanes((LEV, TILE))
-    group_of = lax.rem(lane + 4, TILE) // 8
-
-    @pl.loop(0, FIELDS)
-    def _(f):
-        for side, first in enumerate((4, 20)):
-            for row in range(4):
-                send_x[side, f, row] = st[f, first + row, :, :COLS].astype(BF16)
-
-    def edge(f, row):
-        return jnp.where(lane < 64, st[f, row, :, :TILE], st[f, row, :, COLS - TILE : COLS])
-
-    def pack(group):
-        total = jnp.zeros((LEV, TILE), F32)
-        for j in range(16):
-            part = pltpu.roll(edge(j // 4, 4 + 4 * group + j % 4), 8 * j, 1)
-            total = jnp.where(group_of == j, part, total)
-        send_p[group] = total
-
-    pack(0)
-    pack(4)
-
-    for copy in loads[2 * FIELDS :]:
-        copy.wait()
-    for group in range(1, 4):
-        pack(group)
-
-    pl.semaphore_wait(barrier, 14 + jnp.where(near_edge, 10, 0))
-
-    def copy_x(side, f):
-        where = (sec, low_x, low_y) if side == 0 else (sec, high_x, high_y)
-        return pltpu.make_async_remote_copy(
-            send_x.at[side, f],
-            recv_x.at[1 - side, f],
-            sx_sem.at[side, f],
-            rx_sem.at[1 - side, f],
-            device_id=where,
-            device_id_type=MESH,
-        )
-
-    def copy_p(k):
-        source, target, where = (
-            (send_p, recv_p.at[pl.ds(1, 5)], (other, gx, gy)),
-            (send_p.at[0:1], recv_p.at[pl.ds(6, 1)], (other, low_x, low_y)),
-            (send_p.at[4:5], recv_p.at[pl.ds(0, 1)], (other, high_x, high_y)),
-        )[k]
-        return pltpu.make_async_remote_copy(
-            source, target, sp_sem.at[k], rp_sem.at[k], device_id=where, device_id_type=MESH
-        )
-
-    def copy_l(k):
-        to = lax.rem(gy + k, GY)
-        return pltpu.make_async_remote_copy(
-            send_l.at[to],
-            recv_l.at[gy],
-            sl_sem.at[k],
-            rl_sem.at[gy],
-            device_id=(sec, gx, to),
-            device_id_type=MESH,
-        )
-
-    for k in range(3):
-        copy_p(k).start()
-    for f in range(FIELDS):
-        copy_x(0, f).start()
-        copy_x(1, f).start()
 
     send_l[...] = jnp.zeros_like(send_l)
     for k in range(GY):
@@ -292,22 +292,23 @@
                 recv_p[group], (TILE - 8 * j) % TILE, 1
             )
 
-    copy_p(0).wait_recv()
-    for group in range(1, 6):
-        unpack(group)
-
-    def first_step(f, rows):
+    @pl.loop(0, FIELDS)
+    def _(f):
+        for r in range(4, ROWS + 4):
+            st[f, r, :, COLS:] = jnp.zeros((LEV, TILE), F32)
+
+    def first_step(f, rows, wanted=range(TILES + 1)):
         def emit(r, t, value):
             u[f, r - 2, :, TILE * t : TILE * t + TILE] = value
 
-        stencil(st, coef, band, f, rows, TILES + 1, emit)
-
-    def second_step(f, rows):
+        stencil(st, coef, band, f, rows, wanted, emit)
+
+    def second_step(f, rows, wanted=range(TILES)):
         def emit(r, t, value):
             adv[f, r - 2, :, TILE * t : TILE * t + TILE] = value
             ab[f, r - 2, :, TILE * t : TILE * t + TILE] = value.astype(BF16)
 
-        stencil(u, coef, band, f, rows, TILES, emit)
+        stencil(u, coef, band, f, rows, wanted, emit)
 
     @pl.loop(0, FIELDS)
     def _(f):
@@ -335,6 +336,15 @@
                         dmat[slot, i, tap : tap + LEV, TILE * half : TILE * half + TILE] = taken[
                             first : first + LEV, TILE * b : TILE * b + TILE
                         ]
+
+    copy_p(0).wait_recv()
+    for group in range(1, 6):
+        unpack(group)
+
+    @pl.loop(0, FIELDS)
+    def _(f):
+        first_step(f, range(6, 22), (TILES - 1, TILES, 0))
+        second_step(f, range(6, 18), (TILES - 1, 0))
 
     for f in range(FIELDS):
         take(f, (1, 2), 0)

time: 54.4 us -> 50 us (0.919)
  Pallas kernels: 53.6 us -> 49 us
    pallas_call x1, Pallas kernels: 50.7 us -> 46.2 us  [on_device(): pl.pallas_call(kernel, out_shape=(pltpu.VMEM((FIELDS, ROWS, LEV, COLS), F...]
where the time goes in v3:
time: 50 us; the launch traced here: 49.8 us
  Pallas kernels  49 us (98%)
  between operations  0.8 us (2%)
    pallas_call x1, Pallas kernels, on_device(): pl.pallas_call(kernel, out_shape=(pltpu.VMEM((FIELDS, ROWS, LEV, COLS), F...  46.2 us
    pallas_call x1, Pallas kernels, on_device(): pl.pallas_call(write_out, out_shape=(jax.ShapeDtypeStruct((FIELDS, ROWS,...  2.84 us

profile of v3, /device:TPU:0, one launch (start us, length us, event | category | flops | bytes accessed | tf_op | source)
XLA Modules:
  0.0 49.8 jit_solution(13927091559305096653)
XLA Ops:
  0.6 46.2 %steps_and_fractions.1 = (f32[4,20,16,1280]{3,2,1,0:T(8,128)S(1)}, f32[2,32,32]{2,1,0:T(8,128)S(1)}, f32[2,32,32]{2,1,0:T(8,128)S(1)}) custom-call(f32[4,20,16,1280]{3,2,1,0:T(8,128)} %bitcast.4, f32[4,16]{1,0:T(4,128)} %h_coeff.1, f32[4,16]{1,0:T(4,128)} %v_coeff.1, bf16[5,5,4,32]{3,2,1,0:T(4,128)(2,1)} %bitcast.5, f32[32]{0:T(128)} %conv_bias.1, ...), custom_call_target="tpu_custom_call" | custom-call | tf_op jit(solution)/shard_map/steps_and_fractions/pallas_call | solution.py:506
  46.8 2.8 %write_out.1 = (f32[4,20,16,1280]{3,2,1,0:T(8,128)}, f32[2,32,32]{2,1,0:T(8,128)}, f32[2,32,32]{2,1,0:T(8,128)}) custom-call(f32[4,20,16,1280]{3,2,1,0:T(8,128)S(1)} %get-tuple-element.9.adv, f32[2,32,32]{2,1,0:T(8,128)S(1)} %get-tuple-element.10.column_fraction, f32[2,32,32]{2,1,0:T(8,128)S(1)} %get-tuple-element.11.area_fraction), custom_call_target="tpu_custom_call" | custom-call | tf_op jit(solution)/shard_map/write_out/pallas_call | solution.py:559

commit v4 on v3

--- a/solution.py
+++ b/solution.py
@@ -15,7 +15,6 @@
 COLS = 1280
 TILE = 128
 TILES = COLS // TILE
-WIDE = COLS + TILE
 KERNEL = 5
 CHANNELS = 32
 COARSE = 256
@@ -34,13 +33,15 @@
     return lax.broadcasted_iota(jnp.int32, shape, len(shape) - 2)
 
 
-def stencil(src, coef, band, f, rows, wanted, emit):
+def stencil(src, ends, coef, band, f, rows, wanted, emit):
     lane = lanes((LEV, TILE))
     sub = sublanes((8, TILE))
     tiles = TILES + 1
     needed = sorted({(t + d) % tiles for t in wanted for d in (-1, 0, 1)})
 
     def at(r, t):
+        if t == TILES:
+            return ends[f, r]
         return src[f, r, :, TILE * t : TILE * t + TILE]
 
     parts = []
@@ -90,7 +91,9 @@
     column_out,
     area_out,
     st,
+    st_ends,
     u,
+    u_ends,
     ab,
     coef,
     band,
@@ -133,7 +136,7 @@
         for f in range(FIELDS):
             copy = pltpu.make_async_copy(
                 state.at[f, pl.ds(first, count)],
-                st.at[f, pl.ds(first + 4, count), :, pl.ds(0, COLS)],
+                st.at[f, pl.ds(first + 4, count)],
                 load_sem.at[part, f],
             )
             copy.start()
@@ -173,7 +176,7 @@
     def _(f):
         for side, first in enumerate((4, 20)):
             for row in range(4):
-                send_x[side, f, row] = st[f, first + row, :, :COLS].astype(BF16)
+                send_x[side, f, row] = st[f, first + row].astype(BF16)
 
     pl.semaphore_wait(barrier, 14 + jnp.where(near_edge, 10, 0))
 
@@ -288,27 +291,30 @@
 
     def unpack(group):
         for j in range(16):
-            st[j // 4, 4 * group + j % 4, :, COLS:] = pltpu.roll(
+            st_ends[j // 4, 4 * group + j % 4] = pltpu.roll(
                 recv_p[group], (TILE - 8 * j) % TILE, 1
             )
 
     @pl.loop(0, FIELDS)
     def _(f):
         for r in range(4, ROWS + 4):
-            st[f, r, :, COLS:] = jnp.zeros((LEV, TILE), F32)
+            st_ends[f, r] = jnp.zeros((LEV, TILE), F32)
 
     def first_step(f, rows, wanted=range(TILES + 1)):
         def emit(r, t, value):
-            u[f, r - 2, :, TILE * t : TILE * t + TILE] = value
-
-        stencil(st, coef, band, f, rows, wanted, emit)
+            if t == TILES:
+                u_ends[f, r - 2] = value
+            else:
+                u[f, r - 2, :, TILE * t : TILE * t + TILE] = value
+
+        stencil(st, st_ends, coef, band, f, rows, wanted, emit)
 
     def second_step(f, rows, wanted=range(TILES)):
         def emit(r, t, value):
             adv[f, r - 2, :, TILE * t : TILE * t + TILE] = value
             ab[f, r - 2, :, TILE * t : TILE * t + TILE] = value.astype(BF16)
 
-        stencil(u, coef, band, f, rows, wanted, emit)
+        stencil(u, u_ends, coef, band, f, rows, wanted, emit)
 
     @pl.loop(0, FIELDS)
     def _(f):
@@ -361,7 +367,7 @@
         copy_x(1, f).wait_recv()
         for side, first in enumerate((0, 24)):
             for row in range(4):
-                st[f, first + row, :, :COLS] = recv_x[side, f, row].astype(F32)
+                st[f, first + row] = recv_x[side, f, row].astype(F32)
 
         first_step(f, (2, 3, 4, 5, 22, 23, 24, 25))
         second_step(f, (2, 3, 4, 5, 18, 19, 20, 21))
@@ -513,8 +519,10 @@
         in_specs=[anywhere, vmem, vmem, vmem, smem, smem, smem, vmem, vmem],
         out_specs=(vmem, vmem, vmem),
         scratch_shapes=[
-            pltpu.VMEM((FIELDS, ROWS + 8, LEV, WIDE), F32),
-            pltpu.VMEM((FIELDS, ROWS + 4, LEV, WIDE), F32),
+            pltpu.VMEM((FIELDS, ROWS + 8, LEV, COLS), F32),
+            pltpu.VMEM((FIELDS, ROWS + 8, LEV, TILE), F32),
+            pltpu.VMEM((FIELDS, ROWS + 4, LEV, COLS), F32),
+            pltpu.VMEM((FIELDS, ROWS + 4, LEV, TILE), F32),
             pltpu.VMEM((FIELDS, ROWS, LEV, COLS), BF16),
             pltpu.VMEM((FIELDS, 3, LEV, TILE), F32),
             pltpu.VMEM((2 * TILE, 2 * TILE), BF16),

time: 50 us -> 50.1 us (level)
  no operation moved by 1% of the time
where the time goes in v4:
time: 50.1 us; the launch traced here: 49.9 us
  Pallas kernels  49.1 us (98%)
  between operations  0.8 us (2%)
    pallas_call x1, Pallas kernels, on_device(): pl.pallas_call(kernel, out_shape=(pltpu.VMEM((FIELDS, ROWS, LEV, COLS), F...  46.2 us
    pallas_call x1, Pallas kernels, on_device(): pl.pallas_call(write_out, out_shape=(jax.ShapeDtypeStruct((FIELDS, ROWS,...  2.84 us

profile of v4, /device:TPU:0, one launch (start us, length us, event | category | flops | bytes accessed | tf_op | source)
XLA Modules:
  0.0 49.9 jit_solution(10181964052084229123)
XLA Ops:
  0.6 46.2 %steps_and_fractions.1 = (f32[4,20,16,1280]{3,2,1,0:T(8,128)S(1)}, f32[2,32,32]{2,1,0:T(8,128)S(1)}, f32[2,32,32]{2,1,0:T(8,128)S(1)}) custom-call(f32[4,20,16,1280]{3,2,1,0:T(8,128)} %bitcast.4, f32[4,16]{1,0:T(4,128)} %h_coeff.1, f32[4,16]{1,0:T(4,128)} %v_coeff.1, bf16[5,5,4,32]{3,2,1,0:T(4,128)(2,1)} %bitcast.5, f32[32]{0:T(128)} %conv_bias.1, ...), custom_call_target="tpu_custom_call" | custom-call | tf_op jit(solution)/shard_map/steps_and_fractions/pallas_call | solution.py:512
  46.9 2.8 %write_out.1 = (f32[4,20,16,1280]{3,2,1,0:T(8,128)}, f32[2,32,32]{2,1,0:T(8,128)}, f32[2,32,32]{2,1,0:T(8,128)}) custom-call(f32[4,20,16,1280]{3,2,1,0:T(8,128)S(1)} %get-tuple-element.9.adv, f32[2,32,32]{2,1,0:T(8,128)S(1)} %get-tuple-element.10.column_fraction, f32[2,32,32]{2,1,0:T(8,128)S(1)} %get-tuple-element.11.area_fraction), custom_call_target="tpu_custom_call" | custom-call | tf_op jit(solution)/shard_map/write_out/pallas_call | solution.py:567

commit v5 on v3

--- a/solution.py
+++ b/solution.py
@@ -294,7 +294,7 @@
 
     @pl.loop(0, FIELDS)
     def _(f):
-        for r in range(4, ROWS + 4):
+        for r in range(ROWS + 8):
             st[f, r, :, COLS:] = jnp.zeros((LEV, TILE), F32)
 
     def first_step(f, rows, wanted=range(TILES + 1)):
@@ -337,25 +337,6 @@
                             first : first + LEV, TILE * b : TILE * b + TILE
                         ]
 
-    copy_p(0).wait_recv()
-    for group in range(1, 6):
-        unpack(group)
-
-    @pl.loop(0, FIELDS)
-    def _(f):
-        first_step(f, range(6, 22), (TILES - 1, TILES, 0))
-        second_step(f, range(6, 18), (TILES - 1, 0))
-
-    for f in range(FIELDS):
-        take(f, (1, 2), 0)
-    for i, p in enumerate((1, 2)):
-        feat[p] = jnp.dot(conv_l[...], dmat[0, i], preferred_element_type=F32)
-
-    for k in range(1, 3):
-        copy_p(k).wait_recv()
-    unpack(0)
-    unpack(6)
-    early = 9 * TILE
     for f in range(FIELDS):
         copy_x(0, f).wait_recv()
         copy_x(1, f).wait_recv()
@@ -365,14 +346,22 @@
 
         first_step(f, (2, 3, 4, 5, 22, 23, 24, 25))
         second_step(f, (2, 3, 4, 5, 18, 19, 20, 21))
-        take(f, (0, 3), 1)
-        if f == 2:
-            for i, p in enumerate((0, 3)):
-                feat[p] = jnp.dot(
-                    conv_l[:, :early], dmat[1, i, :early], preferred_element_type=F32
-                )
-    for i, p in enumerate((0, 3)):
-        feat[p] += jnp.dot(conv_l[:, early:], dmat[1, i, early:], preferred_element_type=F32)
+
+    for k in range(3):
+        copy_p(k).wait_recv()
+    for group in range(7):
+        unpack(group)
+
+    @pl.loop(0, FIELDS)
+    def _(f):
+        first_step(f, range(2, 26), (TILES - 1, TILES, 0))
+        second_step(f, range(2, 22), (TILES - 1, 0))
+
+    for slot, pair in enumerate(((1, 2), (0, 3))):
+        for f in range(FIELDS):
+            take(f, pair, slot)
+        for i, p in enumerate(pair):
+            feat[p] = jnp.dot(conv_l[...], dmat[slot, i], preferred_element_type=F32)
 
     for k in range(1, GY):
         pltpu.make_async_remote_copy(

time: 50 us -> 48.4 us (0.968)
  the two profiles are of different devices: /device:TPU:0 before, /device:TPU:1 now
where the time goes in v5:
time: 48.4 us; the launch traced here: 48.2 us
  Pallas kernels  47.4 us (98%)
  between operations  0.8 us (2%)
    pallas_call x1, Pallas kernels, on_device(): pl.pallas_call(kernel, out_shape=(pltpu.VMEM((FIELDS, ROWS, LEV, COLS), F...  44.5 us
    pallas_call x1, Pallas kernels, on_device(): pl.pallas_call(write_out, out_shape=(jax.ShapeDtypeStruct((FIELDS, ROWS,...  2.84 us

profile of v5, /device:TPU:1, one launch (start us, length us, event | category | flops | bytes accessed | tf_op | source)
XLA Modules:
  0.0 48.2 jit_solution(8805694186688329314)
XLA Ops:
  0.6 44.5 %steps_and_fractions.1 = (f32[4,20,16,1280]{3,2,1,0:T(8,128)S(1)}, f32[2,32,32]{2,1,0:T(8,128)S(1)}, f32[2,32,32]{2,1,0:T(8,128)S(1)}) custom-call(f32[4,20,16,1280]{3,2,1,0:T(8,128)} %bitcast.4, f32[4,16]{1,0:T(4,128)} %h_coeff.1, f32[4,16]{1,0:T(4,128)} %v_coeff.1, bf16[5,5,4,32]{3,2,1,0:T(4,128)(2,1)} %bitcast.5, f32[32]{0:T(128)} %conv_bias.1, ...), custom_call_target="tpu_custom_call" | custom-call | tf_op jit(solution)/shard_map/steps_and_fractions/pallas_call | solution.py:495
  45.2 2.8 %write_out.1 = (f32[4,20,16,1280]{3,2,1,0:T(8,128)}, f32[2,32,32]{2,1,0:T(8,128)}, f32[2,32,32]{2,1,0:T(8,128)}) custom-call(f32[4,20,16,1280]{3,2,1,0:T(8,128)S(1)} %get-tuple-element.9.adv, f32[2,32,32]{2,1,0:T(8,128)S(1)} %get-tuple-element.10.column_fraction, f32[2,32,32]{2,1,0:T(8,128)S(1)} %get-tuple-element.11.area_fraction), custom_call_target="tpu_custom_call" | custom-call | tf_op jit(solution)/shard_map/write_out/pallas_call | solution.py:548
